TPU v7x, 256 devices: a whole 4x4x8 slice. The times are simulated.
256 devices in a mesh: dom: 64 (over z, x, core), feat: 4 (over y).
Axes of the slice: x: 4, y: 4, z: 8, core: 2. Of those that a mesh axis runs over, the one named last changes fastest.
Arguments:
- hidden: bfloat16 [256, 262144], P('feat', 'dom'), may hold values from -6 to 6
- tiles: bfloat16 [2048, 12, 128, 128], P('dom')
- tile_src: int32 [2048, 12], P('dom'), may hold values from 0 to 167, as said below
- hub_blocks: int32 [64, 2], P('dom'), may hold values from 0 to 31, as said below
- halo_rows: int32 [64, 64, 16], P('dom'), may hold values from 0 to 4095
- halo_counts: int32 [64, 64], replicated, may hold values from 0 to 16, as said below
- weight_self: bfloat16 [172, 256], P('feat'), may hold values from -0.375 to 0.375
- weight_neigh: bfloat16 [172, 256], P('feat'), may hold values from -0.75 to 0.75
- grad_logits: bfloat16 [172, 262144], P('feat', 'dom'), may hold values from -6 to 6
Outputs:
- logits: bfloat16 [172, 262144], P('feat', 'dom')
- grad_self: float32 [172, 256], P('feat', 'dom')
- grad_neigh: float32 [172, 256], P('feat', 'dom')
- grad_hidden: float32 [256, 262144], P('feat', 'dom')
Inputs may be any that keep to these rules, and one draw needn't show every extreme that they name: `tile_src`: blocks below 32 are the partition's own nodes, the next 8 the received slots, the rest the hub blocks; the first tile of every destination block reads the partition's own nodes. `hub_blocks`: 2 distinct blocks a partition. `halo_counts`: zero where a partition meets itself, at least 1 elsewhere; in every draw some partition receives 16 live slots from every other partition. `halo_rows`: entries beyond the live count of a pair are padding.
All inputs are finite; a program needn't handle non-finite values.
Results may differ from a plain program's by a relative error of at most 0.0035.
Values may be sent and summed in bfloat16 or wider, within the bound.
A program may use at most 128 MiB of HBM per device.

v0:
```python
import jax
import jax.numpy as jnp
from jax import lax
from jax.sharding import PartitionSpec as P

BLK = 128
ROWS_DEV = 4096
TPB = 12
HB = 2
CAP = 16
NB = 32


def local(
    hidden,
    tiles,
    tile_src,
    hub_blocks,
    halo_rows,
    halo_counts,
    weight_self,
    weight_neigh,
    grad_logits,
):
    partitions = lax.axis_size("dom")
    own_index = lax.axis_index("dom")
    columns = hidden.shape[0]
    slot_index = jnp.arange(CAP, dtype=jnp.int32)
    out_counts = lax.dynamic_slice_in_dim(halo_counts, own_index, 1, 0)[0]
    in_counts = lax.dynamic_slice_in_dim(halo_counts, own_index, 1, 1)[:, 0]
    out_alive = (slot_index[None, :] < out_counts[:, None]).astype(jnp.bfloat16)
    in_alive = (slot_index[None, :] < in_counts[:, None]).astype(jnp.float32)
    blocks = hidden.reshape(columns, NB, BLK)
    hub_piece = jnp.take(blocks, hub_blocks[0], axis=1)
    send_rows = halo_rows[0].reshape(-1)
    outgoing = (
        jnp.take(hidden, send_rows, axis=1).reshape(columns, partitions, CAP) * out_alive[None]
    )
    hub_table = lax.all_gather(hub_piece, "dom", axis=1, tiled=True)
    incoming = lax.all_to_all(outgoing, "dom", split_axis=1, concat_axis=1, tiled=True).reshape(
        columns, partitions * CAP
    )
    live_table = jnp.concatenate(
        [
            jnp.ones((ROWS_DEV,), jnp.float32),
            in_alive.reshape(-1),
            jnp.ones((partitions * HB * BLK,), jnp.float32),
        ]
    ).reshape(-1, BLK)
    sources_table = jnp.concatenate(
        [hidden, incoming, hub_table.reshape(columns, -1)], axis=1
    ).reshape(columns, -1, BLK)
    sources = tile_src.reshape(-1)
    picked = jnp.take(sources_table, sources, axis=1).reshape(columns, NB, TPB, BLK)
    summed = jnp.einsum("bjds,cbjs->cbd", tiles, picked, preferred_element_type=jnp.float32)
    live_tiles = jnp.take(live_table, sources, axis=0).reshape(NB, TPB, BLK).astype(jnp.bfloat16)
    degree = jnp.einsum("bjds,bjs->bd", tiles, live_tiles, preferred_element_type=jnp.float32)
    averaged = (summed / degree[None]).reshape(columns, ROWS_DEV).astype(jnp.bfloat16)
    full_hidden, full_mean = (
        lax.all_gather(hidden, "feat", axis=0, tiled=True),
        lax.all_gather(averaged, "feat", axis=0, tiled=True),
    )
    logits = (
        jnp.dot(weight_self, full_hidden, preferred_element_type=jnp.float32)
        + jnp.dot(weight_neigh, full_mean, preferred_element_type=jnp.float32)
    ).astype(jnp.bfloat16)
    factor = float(partitions * ROWS_DEV) ** (-0.5)
    contract_rows = (((1,), (1,)), ((), ()))
    grad_self = (
        lax.dot_general(grad_logits, full_hidden, contract_rows, preferred_element_type=jnp.float32)
        * factor
    )
    grad_neigh = (
        lax.dot_general(grad_logits, full_mean, contract_rows, preferred_element_type=jnp.float32)
        * factor
    )
    contract_classes = (((0,), (0,)), ((), ()))
    direct_full = lax.dot_general(
        weight_self, grad_logits, contract_classes, preferred_element_type=jnp.float32
    )
    spread_full = lax.dot_general(
        weight_neigh, grad_logits, contract_classes, preferred_element_type=jnp.float32
    )
    direct, spread = (
        lax.psum_scatter(direct_full, "feat", scatter_dimension=0, tiled=True),
        lax.psum_scatter(spread_full, "feat", scatter_dimension=0, tiled=True),
    )
    scaled = (spread.reshape(columns, NB, BLK) / degree[None]).astype(jnp.bfloat16)
    pushed = jnp.einsum("bjds,cbd->cbjs", tiles, scaled, preferred_element_type=jnp.float32)
    pushed = pushed.reshape(columns, NB * TPB, BLK)
    returned = (
        jnp.zeros((columns, sources_table.shape[1], BLK), jnp.float32).at[:, sources].add(pushed)
        * live_table[None]
    )
    flattened = returned.reshape(columns, -1)
    own_grad = flattened[:, :ROWS_DEV]
    halo_grad = flattened[:, ROWS_DEV : ROWS_DEV + partitions * CAP].reshape(
        columns, partitions, CAP
    )
    hub_grad = flattened[:, ROWS_DEV + partitions * CAP :].reshape(columns, partitions * HB, BLK)
    hub_sum, grad_self, grad_neigh = (
        lax.psum_scatter(hub_grad, "dom", scatter_dimension=1, tiled=True),
        lax.psum_scatter(grad_self, "dom", scatter_dimension=1, tiled=True),
        lax.psum_scatter(grad_neigh, "dom", scatter_dimension=1, tiled=True),
    )
    sent_back = (
        lax.all_to_all(
            halo_grad.astype(jnp.bfloat16), "dom", split_axis=1, concat_axis=1, tiled=True
        )
        .astype(halo_grad.dtype)
        .reshape(columns, -1)
    )
    own_grad = own_grad.at[:, send_rows].add(sent_back)
    own_grad = (
        own_grad.reshape(columns, NB, BLK)
        .at[:, hub_blocks[0]]
        .add(hub_sum)
        .reshape(columns, ROWS_DEV)
    )
    return (logits, grad_self, grad_neigh, direct + own_grad)


def solution(mesh):
    placed = (
        P("feat", "dom"),
        P("dom", None, None, None),
        P("dom", None),
        P("dom", None),
        P("dom", None, None),
        P(),
        P("feat", None),
        P("feat", None),
        P("feat", "dom"),
    )
    return jax.shard_map(
        local,
        mesh=mesh,
        in_specs=placed,
        out_specs=(P("feat", "dom"), P("feat", "dom"), P("feat", "dom"), P("feat", "dom")),
        check_vma=False,
    )
```

profile of v0, /device:TPU:16, one launch (start us, length us, event | category | flops | bytes accessed | tf_op | source)
XLA Modules:
  0.0 597.5 jit_solution(3211665979421987316)
XLA Ops:
  11.1 1.5 copy.80
  14.3 3.2 gather_fusion
  19.5 11.9 %all-to-all-start = ((bf16[64,2,512]{2,1,0:T(2,128)(2,1)}), bf16[64,2,512]{2,1,0:T(2,128)(2,1)S(1)}, u32[]{:S(2)}, u32[]{:S(2)}) async-start(bf16[64,2,512]{2,1,0:T(2,128)(2,1)} %reshape.286), calls=%async_computation | async-start | bytes 262144 | tf_op jit(solution)/shard_map/all_to_all | solution.py:40
  34.5 6.4 %fusion.20 = f32[32,1,128,1]{2,1,3,0:T(1,128)S(1)} fusion(bf16[32,12,128,128]{3,2,1,0:T(8,128)(2,1)} %param.10, bf16[32,12,128,1]{2,1,0,3:T(8,128)(2,1)S(1)} %fusion.22), kind=kOutput, calls=%fused_computation.39 | convolution fusion | flops 12582912 | bytes 12697600 | tf_op jit(solution)/shard_map/bjds,bjs->bd/dot_general | solution.py:57
  40.9 1.6 all-to-all-done
  42.9 48.5 %all-gather.6.cloned.1.call-done = bf16[64,128,128]{2,0,1:T(8,128)(2,1)} async-done(((bf16[64,2,128]{2,0,1:T(8,128)(2,1)}), bf16[64,128,128]{2,0,1:T(8,128)(2,1)}) %all-gather.6.cloned.1.call-update) | async-done | bytes 2097168 | tf_op jit(solution)/shard_map/all_gather | solution.py:39
  91.4 1.9 copy_bitcast_fusion.3
  93.2 1.8 copy_bitcast_fusion.2
  95.1 13.3 %gather_fusion.2 = bf16[384,64,128]{2,1,0:T(8,128)(2,1)} fusion(bf16[64,168,128]{2,0,1:T(8,128)(2,1)S(1)} %copy_bitcast_fusion.2, s32[1024]{0:T(1024)S(1)} %pad_clamp_fusion), kind=kCustom, calls=%fused_computation.2 | custom fusion | bytes 12584448 | tf_op jit(solution)/shard_map/jit(_take)/gather | solution.py:54
  108.4 11.0 %fusion.13 = bf16[32,8,8,128]{3,2,1,0:T(8,128)(2,1)S(1)} fusion(bf16[32,12,128,128]{3,2,1,0:T(8,128)(2,1)} %param.10, bf16[64,32,12,128]{3,0,2,1:T(8,128)(2,1)} %bitcast.134, pred[32,12]{1,0:T(8,128)(4,1)S(1)} %copy.77, f32[32,128]{1,0:T(8,128)S(1)} %bitcast.140), kind=kOutput, calls=%fused_computation.29 | convolution fusion | flops 808976384 | bytes 19415424 | tf_op jit(solution)/shard_map/bjds,cbjs->cbd/dot_general | solution.py:55
  120.5 2.7 fusion.31
  123.2 3.0 convolution_multiply_fusion
  126.2 32.8 %all-gather.8.cloned.1.call-done = bf16[256,4096]{1,0:T(8,128)(2,1)} async-done(((bf16[64,4096]{1,0:T(8,128)(2,1)}), bf16[256,4096]{1,0:T(8,128)(2,1)}) %all-gather.8.cloned.1.call-update) | async-done | bytes 2097168 | tf_op jit(solution)/shard_map/all_gather | solution.py:61
  159.0 3.0 fusion.9
  162.2 48.3 %reduce-scatter.7.cloned.1.call-done = f32[64,4096]{1,0:T(8,128)} async-done(((f32[256,4096]{1,0:T(8,128)}), f32[64,4096]{1,0:T(8,128)}) %reduce-scatter.7.cloned.1.call-update) | async-done | bytes 1048592 | tf_op jit(solution)/shard_map/reduce_scatter | solution.py:86
  210.6 11.3 %fusion.17 = f32[32,64,12,128]{3,1,2,0:T(8,128)} fusion(bf16[32,12,128,128]{3,2,1,0:T(8,128)(2,1)} %param.10, f32[32,128]{1,0:T(8,128)S(1)} %bitcast.141, f32[64,4096]{1,0:T(8,128)} %reduce-scatter.7.cloned.1.call-done), kind=kOutput, calls=%fused_computation.34 | convolution fusion | flops 805830656 | bytes 26230784 | tf_op jit(solution)/shard_map/bjds,cbd->cbjs/dot_general | solution.py:89
  221.8 3.1 broadcast_in_dim.67
  224.9 59.9 %scatter_fusion = f32[64,168,128]{2,0,1:T(8,128)} fusion(f32[64,168,128]{2,0,1:T(8,128)} %broadcast_in_dim.67, s32[384]{0:T(512)S(1)} %fusion.25, f32[384,64,128]{2,1,0:T(8,128)} %bitcast.132), kind=kCustom, calls=%fused_computation.4 | custom fusion | flops 3145728 | bytes 37750272 | tf_op jit(solution)/shard_map/scatter-add | solution.py:92
  284.8 3.0 copy_bitcast_fusion
  287.8 2.4 copy-done.1
  290.2 2.7 copy_bitcast_fusion.1
  293.7 2.8 fusion.30
  297.7 2.2 fusion.29
  301.9 10.8 %all-to-all-start.1 = ((bf16[64,2,512]{2,1,0:T(2,128)(2,1)}), bf16[64,2,512]{2,1,0:T(2,128)(2,1)}, u32[]{:S(2)}, u32[]{:S(2)}) async-start(bf16[64,2,512]{2,1,0:T(2,128)(2,1)} %reshape.288), calls=%async_computation.3 | async-start | bytes 262144 | tf_op jit(solution)/shard_map/all_to_all | solution.py:107
  312.7 3.0 fusion.4
  315.7 78.1 %all-reduce.5.cloned.1.call-done = (f32[43,256]{0,1:T(8,128)}, f32[43,256]{1,0:T(8,128)}) async-done(((f32[43,256]{0,1:T(8,128)}, f32[43,256]{1,0:T(8,128)}), (f32[43,256]{0,1:T(8,128)}, f32[43,256]{1,0:T(8,128)})) %all-reduce.5.cloned.1.call-update) | async-done | bytes 88080
  395.3 1.3 constant_dynamic-slice_fusion.1
  398.3 6.8 %scatter_custom_fusion.1 = f32[64,4096]{0,1:T(8,128)S(1)} fusion(f32[64,4096]{0,1:T(8,128)S(1)} %copy.101, s32[1024]{0:T(1024)S(1)} %bitcast.144, bf16[64,1024]{0,1:T(8,128)(2,1)S(1)} %bitcast.136), kind=kCustom, calls=%fused_computation.33 | custom fusion | flops 131072 | bytes 1310720 | tf_op jit(solution)/shard_map/scatter-add | solution.py:113
  405.8 133.9 %reduce-scatter.9.cloned.1.call-done = f32[64,2,128]{2,0,1:T(8,128)} async-done(((f32[64,128,128]{2,0,1:T(8,128)}), f32[64,2,128]{2,0,1:T(8,128)}) %reduce-scatter.9.cloned.1.call-update) | async-done | bytes 65552 | tf_op jit(solution)/shard_map/reduce_scatter | solution.py:102
  539.7 1.4 scatter_fusion.1
  541.1 47.2 %reduce-scatter.5.cloned.1.call-done = f32[64,4096]{1,0:T(8,128)} async-done(((f32[256,4096]{1,0:T(8,128)}), f32[64,4096]{1,0:T(8,128)}) %reduce-scatter.5.cloned.1.call-update) | async-done | bytes 1048592 | tf_op jit(solution)/shard_map/reduce_scatter | solution.py:85
  588.3 2.3 bitcast_add_fusion
  (76 shorter events, 19.2 us)
Async XLA Ops:
  7.2 113.3 %copy-start = (bf16[43,4096]{1,0:T(8,128)(2,1)S(1)}, bf16[43,4096]{1,0:T(8,128)(2,1)}, u32[]{:S(2)}) copy-start(bf16[43,4096]{1,0:T(8,128)(2,1)} %param.17) | copy-start | bytes 1056772
  7.2 25.2 %copy-start.6 = (s32[64,64]{1,0:T(8,128)S(1)}, s32[64,64]{1,0:T(8,128)}, u32[]{:S(2)}) copy-start(s32[64,64]{1,0:T(8,128)} %param.14) | copy-start | bytes 49156
  7.2 25.4 %copy-start.5 = (s32[32,12]{0,1:T(8,128)S(1)}, s32[32,12]{0,1:T(8,128)}, u32[]{:S(2)}) copy-start(s32[32,12]{0,1:T(8,128)} %param.11) | copy-start | bytes 4612
  7.2 84.2 %all-gather.6.cloned.1.call-start = ((), (), s32[]{:S(2)}) async-start(), calls=%async_computation.6 | async-start | bytes 2129920 | tf_op jit(solution)/shard_map/all_gather | solution.py:39
  19.5 23.0 %all-to-all-start = ((bf16[64,2,512]{2,1,0:T(2,128)(2,1)}), bf16[64,2,512]{2,1,0:T(2,128)(2,1)S(1)}, u32[]{:S(2)}, u32[]{:S(2)}) async-start(bf16[64,2,512]{2,1,0:T(2,128)(2,1)} %reshape.286), calls=%async_computation | async-start | bytes 262144 | tf_op jit(solution)/shard_map/all_to_all | solution.py:40
  31.4 91.8 %all-gather.4.cloned.1.call-start = ((), (), s32[]{:S(2)}) async-start(), calls=%async_computation.5 | async-start | bytes 2621440 | tf_op jit(solution)/shard_map/all_gather | solution.py:60
  32.2 126.8 %all-gather.8.cloned.1.call-start = ((), (), s32[]{:S(2)}) async-start(), calls=%async_computation.7 | async-start | bytes 2621440 | tf_op jit(solution)/shard_map/all_gather | solution.py:61
  108.4 12.0 %copy-start.4 = (bf16[43,256]{1,0:T(8,128)(2,1)S(1)}, bf16[43,256]{1,0:T(8,128)(2,1)}, u32[]{:S(2)}) copy-start(bf16[43,256]{1,0:T(8,128)(2,1)} %param.16) | copy-start | bytes 66052
  120.4 90.2 %reduce-scatter.7.cloned.1.call-start = ((), (), s32[]{:S(2)}) async-start(), calls=%async_computation.9 | async-start | bytes 5242880 | tf_op jit(solution)/shard_map/reduce_scatter | solution.py:86
  123.2 270.7 %all-reduce.5.cloned.1.call-start = ((), (), s32[]{:S(2)}) async-start(), calls=%async_computation.11 | async-start | bytes 360448
  162.0 377.7 %reduce-scatter.9.cloned.1.call-start = ((), (), s32[]{:S(2)}) async-start(), calls=%async_computation.10 | async-start | bytes 4259840 | tf_op jit(solution)/shard_map/reduce_scatter | solution.py:102
  287.8 2.4 copy-start.1
  292.9 0.7 copy-start.3
  293.0 3.5 copy-start.7
  293.0 4.7 copy-start.2
  293.0 295.4 %reduce-scatter.5.cloned.1.call-start = ((), (), s32[]{:S(2)}) async-start(), calls=%async_computation.8 | async-start | bytes 5242880 | tf_op jit(solution)/shard_map/reduce_scatter | solution.py:85
  297.7 98.8 %slice-start = ((f32[64,21504]{1,0:T(8,128)}), f32[64,4096]{1,0:T(8,128)S(1)}, s32[]{:S(2)}) async-start(f32[64,21504]{1,0:T(8,128)} %copy-done.1), calls=%async_computation.12 | async-start | bytes 2097152 | tf_op jit(solution)/shard_map/slice | solution.py:96
  301.9 95.3 %all-to-all-start.1 = ((bf16[64,2,512]{2,1,0:T(2,128)(2,1)}), bf16[64,2,512]{2,1,0:T(2,128)(2,1)}, u32[]{:S(2)}, u32[]{:S(2)}) async-start(bf16[64,2,512]{2,1,0:T(2,128)(2,1)} %reshape.288), calls=%async_computation.3 | async-start | bytes 262144 | tf_op jit(solution)/shard_map/all_to_all | solution.py:107
Sparse Core Ops, SparseCore 0:
  11.4 79.9 all-gather.5
  93.2 29.8 all-gather.3
  125.5 33.4 all-gather.7
  161.4 49.1 reduce-scatter.6
  214.3 179.4 all-reduce.4
  398.4 141.2 reduce-scatter.8
  542.2 46.0 reduce-scatter.4
where the time goes:
time: 602 us; the launch traced here: 597 us
  waiting for transfers between devices  391 us (65%)
  other arithmetic  78.8 us (13%)
  matrix products  45.2 us (8%)
  local copies, waits for them, and re-layouts  43.6 us (7%)
  starting transfers between devices  23.4 us (4%)
  between operations  15.2 us (3%)
    reduce_scatter x1, waiting for transfers between devices, local(): lax.psum_scatter(hub_grad, 'dom', scatter_dimension=1, tiled=True)  134 us
    unnamed x8, waiting for transfers between devices  78.9 us
    scatter-add x1, other arithmetic, local(): jnp.zeros((columns, sources_table.shape[1], BLK), jnp.float32)  59.9 us
    all_gather x1, waiting for transfers between devices, local(): hub_table = lax.all_gather(hub_piece, 'dom', axis=1, tiled=True)  48.5 us
    reduce_scatter x1, waiting for transfers between devices, local(): lax.psum_scatter(spread_full, 'feat', scatter_dimension=0, tiled=True)  48.3 us
    reduce_scatter x1, waiting for transfers between devices, local(): lax.psum_scatter(direct_full, 'feat', scatter_dimension=0, tiled=True)  47.2 us
    all_gather x1, waiting for transfers between devices, local(): lax.all_gather(averaged, 'feat', axis=0, tiled=True)  32.8 us
    gather x1, local copies, waits for them, and re-layouts, local(): jnp.take(sources_table, sources, axis=1).reshape(columns, NB, TPB, BLK)  13.3 us
  transfers between devices with their start and end apart: 9, of which 7 were waited for; matrix products, arithmetic and copies ran while one was open for 27% of the time, Pallas kernels for 0%

commit v1 on v0

v1 whole, which is shorter than its diff:
```python
import jax
import jax.numpy as jnp
from jax import lax
from jax.experimental import pallas as pl
from jax.experimental.pallas import tpu as pltpu
from jax.sharding import PartitionSpec as P

BF = jnp.bfloat16
F32 = jnp.float32
BLK = 128
ROWS_DEV = 4096
TPB = 12
HB = 2
CAP = 16
NB = 32
NZ, NX, NC, NF = 8, 4, 2, 4
PARTS = NZ * NX * NC
GR = 43
GP = 48
FD = 64
EXT = 168
TR = 80
VM = pltpu.VMEM
CHUNK = 512
NT = (((1,), (1,)), ((), ()))
TN = (((0,), (0,)), ((), ()))


def spec(space=pltpu.VMEM):
    return pl.BlockSpec(memory_space=space)


def one_hot_rows(rows, start, size):
    node = lax.broadcasted_iota(jnp.int32, (size, PARTS * CAP), 0) + start
    return (node == rows).astype(F32).astype(BF)


def prep_kernel(hub_ref, hidden_ref, rows_ref, halo_ref, hubs_ref, total):
    core = lax.rem(lax.axis_index("dom"), NC)
    for i in range(HB):
        start = pl.multiple_of(hub_ref[0, i] * BLK, BLK)
        hubs_ref[i] = hidden_ref[:, pl.ds(start, BLK)]
    rows = rows_ref[...]
    total[...] = jnp.zeros_like(total)

    @pl.loop(0, ROWS_DEV // CHUNK)
    def _(i):
        start = pl.multiple_of(i * CHUNK, CHUNK)
        hot = one_hot_rows(rows, start, CHUNK)
        total[...] += jnp.dot(hidden_ref[:, pl.ds(start, CHUNK)], hot, preferred_element_type=F32)

    for k in range(NZ):
        piece = total[:, k * BLK : (k + 1) * BLK]
        zero = jnp.zeros_like(piece)
        both = jnp.concatenate(
            [jnp.where(core == 0, piece, zero), jnp.where(core == 1, piece, zero)], axis=0
        )
        halo_ref[k] = both.T.astype(BF).reshape(NX, NC, CAP, BLK)


def prep(hub_blocks, hidden, rows):
    return pl.pallas_call(
        prep_kernel,
        out_shape=(
            jax.ShapeDtypeStruct((NZ, NX, NC, CAP, BLK), BF),
            jax.ShapeDtypeStruct((HB, FD, BLK), BF),
        ),
        in_specs=[spec(pltpu.SMEM), spec(), spec()],
        out_specs=(spec(), spec()),
        scratch_shapes=[VM((FD, PARTS * CAP), F32)],
        compiler_params=pltpu.CompilerParams(vmem_limit_bytes=32 << 20),
    )(hub_blocks, hidden, rows)


def slot_place():
    row = lax.broadcasted_iota(jnp.int32, (NX * CAP, NC * BLK), 0)
    lane = lax.broadcasted_iota(jnp.int32, (NX * CAP, NC * BLK), 1)
    want = (row // CAP) * (NC * CAP) + (lane // BLK) * CAP + row % CAP
    return (lane % BLK == want).astype(F32).astype(BF)


def layer_kernel(
    src_ref,
    tiles_ref,
    hidden_ref,
    halo_ref,
    hubs_ref,
    counts_ref,
    gl_ref,
    w_ref,
    own_ref,
    back_ref,
    hubg_ref,
    part_ref,
    mine_ref,
    pg_ref,
    table,
    live,
    acc,
    wt,
    logit,
    grads,
):
    step = pl.program_id(0)
    dom = lax.axis_index("dom")
    feat = lax.axis_index("feat")

    @pl.when(step == 0)
    def _():
        acc[...] = jnp.zeros_like(acc)
        grads[...] = jnp.zeros_like(grads)
        wt[...] = w_ref[...].reshape(NF * GP, 2 * FD).astype(F32).T.astype(BF)
        rows = TR - FD
        first = (lax.broadcasted_iota(jnp.int32, (rows, BLK), 0) == 0).astype(F32)
        ones = first.astype(BF)
        pick = (lax.broadcasted_iota(jnp.int32, (16, PARTS), 1) == dom).astype(F32).astype(BF)
        got = lax.dot_general(
            pick, counts_ref[...].astype(F32).astype(BF), NT, preferred_element_type=F32
        )
        sender = lax.broadcasted_iota(jnp.int32, (PARTS, PARTS * CAP), 0)
        column = lax.broadcasted_iota(jnp.int32, (PARTS, PARTS * CAP), 1)
        spread_out = (column // CAP == sender).astype(F32).astype(BF)
        limit = jnp.dot(got.astype(BF), spread_out, preferred_element_type=F32)
        slot = lax.broadcasted_iota(jnp.int32, (16, PARTS * CAP), 1) % CAP
        live[...] = (slot.astype(F32) < limit).astype(F32)
        for b in range(NB):
            table[b, 0:FD] = hidden_ref[:, b * BLK : (b + 1) * BLK]
            table[b, FD:TR] = ones
        place = slot_place()
        for z in range(NZ):
            rows_z = halo_ref[:, z].reshape(NX * CAP, BLK)
            res = lax.dot_general(rows_z, place, TN, preferred_element_type=F32)
            alive = live[0:1, z * BLK : (z + 1) * BLK]
            block = (res[0:FD, 0:BLK] + res[FD:, BLK:]) * alive
            table[NB + z, 0:FD] = block.astype(BF)
            table[NB + z, FD:TR] = (first * alive).astype(BF)

        @pl.loop(0, PARTS * HB)
        def _(h):
            table[NB + NZ + h, 0:FD] = hubs_ref[h]
            table[NB + NZ + h, FD:TR] = ones

    span = pl.ds(pl.multiple_of(step * (2 * BLK), 2 * BLK), 2 * BLK)
    gl = gl_ref[:, :, span].reshape(NF * GP, 2 * BLK)
    both = jnp.dot(wt[...], gl, preferred_element_type=F32)
    means = []
    for k in range(2):
        b = step * 2 + k
        picks = [src_ref[b, j] for j in range(TPB)]
        weights = jnp.concatenate([tiles_ref[k, j] for j in range(TPB)], axis=1)
        picked = jnp.concatenate([table[picks[j]] for j in range(TPB)], axis=1)
        summed = lax.dot_general(picked, weights, NT, preferred_element_type=F32)
        degree = summed[FD : FD + 1]
        means.append((summed[0:FD] / degree).astype(BF))
        lanes = slice(k * BLK, (k + 1) * BLK)
        scaled = (both[FD:, lanes] / degree).astype(BF)
        acc[b] += both[0:FD, lanes]
        pushed = jnp.dot(scaled, weights, preferred_element_type=F32)
        for j in range(TPB):
            acc[picks[j]] += pushed[:, j * BLK : (j + 1) * BLK]
    x = jnp.concatenate([hidden_ref[:, span], jnp.concatenate(means, axis=1)], axis=0)
    logit[...] = jnp.dot(
        w_ref[...].reshape(NF * GP, 2 * FD), x, preferred_element_type=F32
    ).reshape(NF, GP, 2 * BLK)
    part_ref[:, :, span] = logit[...].astype(BF)
    mine_ref[:, span] = logit[feat]
    grads[...] += lax.dot_general(x, gl, NT, preferred_element_type=F32)

    @pl.when(step == NB // 2 - 1)
    def _():
        for b in range(NB):
            own_ref[:, b * BLK : (b + 1) * BLK] = acc[b]
        place = slot_place()
        for z in range(NZ):
            block = (acc[NB + z] * live[0:1, z * BLK : (z + 1) * BLK]).astype(BF)
            zero = jnp.zeros_like(block)
            wide = jnp.concatenate(
                [jnp.concatenate([block, zero], axis=1), jnp.concatenate([zero, block], axis=1)],
                axis=0,
            )
            back = lax.dot_general(place, wide, NT, preferred_element_type=F32)
            back_ref[:, z] = back.astype(BF).reshape(NX, CAP, BLK)

        @pl.loop(0, PARTS * HB)
        def _(h):
            hubg_ref[h] = acc[NB + NZ + h].astype(BF)

        total = grads[...] * float(PARTS * ROWS_DEV) ** (-0.5)
        for j in range(16):
            pair = jnp.concatenate([total[4 * j : 4 * j + 4], total[FD + 4 * j : FD + 4 * j + 4]], axis=0)
            for f in range(NF):
                pg_ref[f, j] = jnp.concatenate(
                    [pair[:, f * GP : (f + 1) * GP], jnp.zeros((8, BLK - GP), F32)], axis=1
                )


def layer(src, tiles, hidden, halo, hubs, counts, gl, w):
    outs = (
        jax.ShapeDtypeStruct((FD, ROWS_DEV), F32),
        jax.ShapeDtypeStruct((NX, NZ, CAP, BLK), BF),
        jax.ShapeDtypeStruct((PARTS * HB, FD, BLK), BF),
        jax.ShapeDtypeStruct((NF, GP, ROWS_DEV), BF),
        jax.ShapeDtypeStruct((GP, ROWS_DEV), F32),
        jax.ShapeDtypeStruct((NF, 16, 8, BLK), F32),
    )
    return pl.pallas_call(
        layer_kernel,
        grid=(NB // 2,),
        out_shape=outs,
        in_specs=[
            spec(pltpu.SMEM),
            pl.BlockSpec((2, TPB, BLK, BLK), lambda i: (i, 0, 0, 0)),
        ]
        + [spec()] * 6,
        out_specs=(spec(),) * 6,
        scratch_shapes=[
            VM((EXT, TR, BLK), BF),
            VM((16, PARTS * CAP), F32),
            VM((EXT, FD, BLK), F32),
            VM((2 * FD, NF * GP), BF),
            VM((NF, GP, 2 * BLK), F32),
            VM((2 * FD, NF * GP), F32),
        ],
        compiler_params=pltpu.CompilerParams(vmem_limit_bytes=56 << 20),
    )(src, tiles, hidden, halo, hubs, counts, gl, w)


def finish_kernel(hub_ref, own_ref, rows_ref, first_ref, second_ref, sum_ref, out_ref):
    core = lax.rem(lax.axis_index("dom"), NC)
    flat = []
    for k in range(NZ * NX // 4):
        a = first_ref[pl.ds(4 * k, 4)]
        b = second_ref[pl.ds(4 * k, 4)]
        turned = jnp.stack([a, b], axis=1).reshape(BLK, BLK).astype(F32).T
        flat.append(jnp.where(core == 0, turned[0:FD], turned[FD:]).astype(BF))
    back = jnp.concatenate(flat, axis=1)
    rows = rows_ref[...]

    @pl.loop(0, ROWS_DEV // CHUNK)
    def _(i):
        start = pl.multiple_of(i * CHUNK, CHUNK)
        hot = one_hot_rows(rows, start, CHUNK)
        got = lax.dot_general(back, hot, NT, preferred_element_type=F32)
        out_ref[:, pl.ds(start, CHUNK)] = own_ref[:, pl.ds(start, CHUNK)] + got

    for i in range(HB):
        start = pl.multiple_of(hub_ref[0, i] * BLK, BLK)
        out_ref[:, pl.ds(start, BLK)] += sum_ref[i]


def finish(hub_blocks, own, rows, first, second, hub_sum):
    return pl.pallas_call(
        finish_kernel,
        out_shape=jax.ShapeDtypeStruct((FD, ROWS_DEV), F32),
        in_specs=[spec(pltpu.SMEM)] + [spec()] * 5,
        out_specs=spec(),
        compiler_params=pltpu.CompilerParams(vmem_limit_bytes=32 << 20),
    )(hub_blocks, own, rows, first, second, hub_sum)


def local(
    hidden,
    tiles,
    tile_src,
    hub_blocks,
    halo_rows,
    halo_counts,
    weight_self,
    weight_neigh,
    grad_logits,
):
    rows = halo_rows.reshape(1, PARTS * CAP)
    halo_out, hub_piece = prep(hub_blocks, hidden, rows)
    pad = ((0, GP - GR), (0, 0))
    hubs = lax.all_gather(hub_piece, "dom", axis=0, tiled=True)
    gl = lax.all_gather(jnp.pad(grad_logits, pad), "feat", axis=0, tiled=False)
    w = jnp.stack(
        [weight_self.reshape(GR, NF, FD), weight_neigh.reshape(GR, NF, FD)], axis=2
    ).reshape(GR, NF, 2 * FD)
    w = jnp.pad(w.transpose(1, 0, 2), ((0, 0), (0, GP - GR), (0, 0)))
    w = lax.all_to_all(w, "feat", 0, 0, tiled=True)
    halo = lax.all_to_all(halo_out.reshape(PARTS, CAP, BLK), "dom", 0, 0, tiled=True)
    halo = halo.reshape(NZ, NX, NC, CAP, BLK).sum(axis=2).transpose(1, 0, 2, 3)
    own, back, hubg, part, mine, pg = layer(
        tile_src, tiles, hidden, halo, hubs, halo_counts, gl, w
    )
    parts = lax.all_to_all(part, "feat", 0, 0, tiled=True)
    feat = lax.axis_index("feat")
    others = jnp.arange(NF)[:, None, None] != feat
    logits = (mine + jnp.where(others, parts.astype(F32), 0.0).sum(axis=0))[:GR].astype(BF)
    hub_sum = lax.psum_scatter(hubg.astype(F32), "dom", scatter_dimension=0, tiled=True)
    pg = lax.psum_scatter(pg.reshape(PARTS, 8, BLK), "dom", scatter_dimension=0, tiled=True)[0]
    moves = [
        ((16 * g + j) * NF + f, (16 * f + j) * NF + g)
        for g in range(NF)
        for j in range(16)
        for f in range(NF)
    ]
    pg = lax.ppermute(pg, ("dom", "feat"), moves)
    grad_self, grad_neigh = pg[:4, :GR].T, pg[4:, :GR].T
    back = jnp.broadcast_to(back.transpose(1, 0, 2, 3)[:, :, None], (NZ, NX, NC, CAP, BLK))
    back = lax.all_to_all(back.reshape(PARTS, CAP, BLK), "dom", 0, 0, tiled=True)
    back = back.reshape(NZ * NX, NC, CAP, BLK)
    grad_hidden = finish(hub_blocks, own, rows, back[:, 0], back[:, 1], hub_sum)
    return logits, grad_self, grad_neigh, grad_hidden


def solution(mesh):
    placed = (
        P("feat", "dom"),
        P("dom", None, None, None),
        P("dom", None),
        P("dom", None),
        P("dom", None, None),
        P(),
        P("feat", None),
        P("feat", None),
        P("feat", "dom"),
    )
    return jax.shard_map(
        local,
        mesh=mesh,
        in_specs=placed,
        out_specs=(P("feat", "dom"), P("feat", "dom"), P("feat", "dom"), P("feat", "dom")),
        check_vma=False,
    )
```

time: 602 us -> 483 us (0.80)
  other arithmetic: 78.8 us -> 5.47 us
  matrix products: 45.2 us -> 0 us
  Pallas kernels: 0 us -> 35.3 us
  local copies, waits for them, and re-layouts: 43.6 us -> 11.8 us
  waiting for transfers between devices: 391 us -> 369 us
  blocking collectives: 0 us -> 19.6 us
    reduce_scatter x3 -> x1, waiting for transfers between devices: 229 us -> 131 us  [local(): lax.psum_scatter(hubg.astype(F32), 'dom', scatter_dimension=0, tiled=True)]
    scatter-add x3 -> x0, other arithmetic: 68.2 us -> none  [the longest x1 59.9 us: local(): jnp.zeros((columns, sources_table.shape[1], BLK), jnp.float32)]
    unnamed x8 -> x5, waiting for transfers between devices: 78.9 us -> 144 us
    dot_general x9 -> x0, matrix products: 45.2 us -> none  [the longest x1 11.3 us: local(): jnp.einsum('bjds,cbd->cbjs', tiles, scaled, preferred_element_type=jnp.fl...]
    pallas_call x0 -> x3, Pallas kernels: none -> 35.3 us  [the longest x1 26.3 us: layer(): pl.pallas_call(layer_kernel, grid=(NB // 2,), out_shape=outs, in_specs=[s...]
    all_to_all x0 -> x1, blocking collectives: none -> 19.6 us  [local(): lax.all_to_all(back.reshape(PARTS, CAP, BLK), 'dom', 0, 0, tiled=True)]
    gather x5 -> x0, local copies, waits for them, and re-layouts: 18.3 us -> none  [the longest x1 13.3 us: local(): jnp.take(sources_table, sources, axis=1).reshape(columns, NB, TPB, BLK)]
    all_to_all x2 -> x3, waiting for transfers between devices: 1.62 us -> 13.4 us  [the longest x1 11 us: local(): lax.all_to_all(halo_out.reshape(PARTS, CAP, BLK), 'dom', 0, 0, tiled=True)]
  transfers between devices with their start and end apart: 9 -> 8, of which waited for: 7 -> 6; matrix products, arithmetic and copies ran while one was open for 27% -> 2% of each run, Pallas kernels for 0% -> 1%
where the time goes in v1:
time: 483 us; the launch traced here: 482 us
  waiting for transfers between devices  369 us (76%)
  Pallas kernels  35.3 us (7%)
  starting transfers between devices  26.5 us (5%)
  blocking collectives  19.6 us (4%)
  between operations  13.9 us (3%)
  local copies, waits for them, and re-layouts  11.8 us (2%)
  other arithmetic  5.47 us (1%)
    unnamed x5, waiting for transfers between devices  144 us
    reduce_scatter x1, waiting for transfers between devices, local(): lax.psum_scatter(hubg.astype(F32), 'dom', scatter_dimension=0, tiled=True)  131 us
    all_gather x1, waiting for transfers between devices, local(): hubs = lax.all_gather(hub_piece, 'dom', axis=0, tiled=True)  74.1 us
    pallas_call x1, Pallas kernels, layer(): pl.pallas_call(layer_kernel, grid=(NB // 2,), out_shape=outs, in_specs=[s...  26.3 us
    all_to_all x1, blocking collectives, local(): lax.all_to_all(back.reshape(PARTS, CAP, BLK), 'dom', 0, 0, tiled=True)  19.6 us
    all_to_all x1, starting transfers between devices, local(): lax.all_to_all(halo_out.reshape(PARTS, CAP, BLK), 'dom', 0, 0, tiled=True)  11.9 us
    all_to_all x1, waiting for transfers between devices, local(): lax.all_to_all(halo_out.reshape(PARTS, CAP, BLK), 'dom', 0, 0, tiled=True)  11 us
  transfers between devices with their start and end apart: 8, of which 6 were waited for; matrix products, arithmetic and copies ran while one was open for 2% of the time, Pallas kernels for 1%

profile of v1, /device:TPU:16, one launch (start us, length us, event | category | flops | bytes accessed | tf_op | source)
XLA Modules:
  0.0 481.9 jit_solution(13917149856400642126)
XLA Ops:
  7.2 1.8 pad.8
  9.1 0.8 copy.26
  10.0 1.0 copy-done
  11.0 0.7 copy-done.3
  11.7 3.8 shard_map.120
  15.5 11.9 %all-to-all-start = ((bf16[64,16,128]{2,1,0:T(8,128)(2,1)}), bf16[64,16,128]{2,1,0:T(8,128)(2,1)S(1)}, u32[]{:S(2)}, u32[]{:S(2)}) async-start(bf16[64,16,128]{2,1,0:T(8,128)(2,1)} %bitcast), calls=%async_computation | async-start | bytes 524288 | tf_op jit(solution)/shard_map/all_to_all | solution.py:282
  27.5 0.7 copy.31.src_ref
  28.4 0.2 pad_maximum_fusion
  28.6 0.1 reshape.38
  28.8 0.6 pad.9
  29.4 11.0 %all-to-all-done = bf16[64,16,128]{2,1,0:T(8,128)(2,1)S(1)} async-done(((bf16[64,16,128]{2,1,0:T(8,128)(2,1)}), bf16[64,16,128]{2,1,0:T(8,128)(2,1)S(1)}, u32[]{:S(2)}, u32[]{:S(2)}) %all-to-all-start) | async-done | bytes 262176 | tf_op jit(solution)/shard_map/all_to_all | solution.py:282
  40.4 4.8 all-to-all-start.1
  45.3 0.7 copy.39
  45.9 2.3 all-to-all-done.1.w_ref
  48.3 74.1 %all-gather.4.cloned.1.call-done.hubs_ref = bf16[128,64,128]{2,1,0:T(8,128)(2,1)} async-done(((bf16[2,64,128]{2,1,0:T(8,128)(2,1)}), bf16[128,64,128]{2,1,0:T(8,128)(2,1)}) %all-gather.4.cloned.1.call-update) | async-done | bytes 2097168 | tf_op jit(solution)/shard_map/all_gather | solution.py:275
  122.4 26.3 %shard_map.121 = (f32[64,4096]{1,0:T(8,128)}, bf16[4,8,16,128]{3,2,1,0:T(8,128)(2,1)}, bf16[128,64,128]{2,1,0:T(8,128)(2,1)}, bf16[4,48,4096]{2,1,0:T(8,128)(2,1...) custom-call(s32[32,12]{1,0:T(8,128)} %copy.31.src_ref, bf16[32,12,128,128]{3,2,1,0:T(8,128)(2,1)} %tiles_ref.1, ...), custom_call_target="tpu_custom_call" | custom-call | tf_op jit(solution)/shard_map/pallas_call | solution.py:206
  148.7 4.0 convert_element_type.14
  152.7 0.9 copy-done.7
  153.7 19.6 %all_to_all.20 = bf16[64,16,128]{2,1,0:T(8,128)(2,1)S(1)} all-to-all(bf16[64,16,128]{2,1,0:T(8,128)(2,1)S(1)} %bitcast.31), channel_id=1, replica_groups=mesh['dom'=64,'feat'=4] {'dom'}, dimensions={0} | all-to-all | bytes 524288 | tf_op jit(solution)/shard_map/all_to_all | solution.py:302
  173.3 4.8 all-to-all-start.2
  178.1 0.6 dynamic-slice
  178.7 143.4 %all-reduce.5.cloned.1.call-done = f32[64,8,128]{2,1,0:T(8,128)} async-done(((f32[64,8,128]{2,1,0:T(8,128)}), f32[64,8,128]{2,1,0:T(8,128)}) %all-reduce.5.cloned.1.call-update) | async-done | bytes 262160
  322.2 1.3 dynamic-slice_bitcast_fusion
  323.5 4.8 %collective-permute-start = (f32[8,128]{1,0:T(8,128)S(1)}, f32[8,128]{1,0:T(8,128)S(1)}, u32[]{:S(2)}, u32[]{:S(2)}) collective-permute-start(f32[8,128]{1,0:T(8,128)S(1)} %dynamic-slice_bitcast_fusion), channel_id=1, source_target_pairs={{0,0},{1,64},{2,128},{3,192},{4,4},{5,68},{6,132},{7,196},{8,8},{9... | collective-permute-start | bytes 12296 | tf_op jit(solution)/shard_map/ppermute | solution.py:299
  328.4 6.9 %collective-permute-done = f32[8,128]{1,0:T(8,128)S(1)} collective-permute-done((f32[8,128]{1,0:T(8,128)S(1)}, f32[8,128]{1,0:T(8,128)S(1)}, u32[]{:S(2)}, u32[]{:S(2)}) %collective-permute-start) | collective-permute-done | bytes 4128 | tf_op jit(solution)/shard_map/ppermute | solution.py:299
  335.3 0.6 slice_bitcast_fusion.2
  335.9 0.4 select_reduce_fusion
  336.3 0.8 copy-done.5
  337.2 0.8 fusion
  338.0 131.3 %reduce-scatter.2.cloned.1.call-done.sum_ref = f32[2,64,128]{2,1,0:T(8,128)} async-done(((f32[128,64,128]{2,1,0:T(8,128)}), f32[2,64,128]{2,1,0:T(8,128)}) %reduce-scatter.2.cloned.1.call-update) | async-done | bytes 65552 | tf_op jit(solution)/shard_map/reduce_scatter | solution.py:291
  469.3 0.8 copy-done.2
  470.1 5.2 %shard_map.122 = f32[64,4096]{1,0:T(8,128)} custom-call(s32[1,2]{1,0:T(1,128)S(1)} %copy-done.4, f32[64,4096]{1,0:T(8,128)S(1)} %copy-done.1, s32[1,1024]{1,0:T(1,128)S(1)} %reshape.35.rows_ref, bf16[32,16,128]{2,1,0:T(8,128)(2,1)S(1)} %get-tuple-element.21.first_ref, bf16[32,16,128]{2,1,0:T(8,128)(2,1)S(1)} %get-tuple-element.20.second_ref, ...), custom_call_target="tpu_custom_call" | custom-call | tf_op jit(solution)/shard_map/pallas_call | solution.py:252
  (38 shorter events, 0.6 us)
Async XLA Ops:
  7.2 20.3 %copy-start.10 = (s32[32,12]{0,1:T(8,128)S(1)}, s32[32,12]{0,1:T(8,128)}, u32[]{:S(2)}) copy-start(s32[32,12]{0,1:T(8,128)} %param.11) | copy-start | bytes 4612
  7.2 21.0 %copy-start.8 = (bf16[43,256]{1,0:T(8,128)(2,1)S(1)}, bf16[43,256]{1,0:T(8,128)(2,1)}, u32[]{:S(2)}) copy-start(bf16[43,256]{1,0:T(8,128)(2,1)} %param.16) | copy-start | bytes 66052
  7.2 21.1 %copy-start.9 = (bf16[43,256]{1,0:T(8,128)(2,1)S(1)}, bf16[43,256]{1,0:T(8,128)(2,1)}, u32[]{:S(2)}) copy-start(bf16[43,256]{1,0:T(8,128)(2,1)} %param.15) | copy-start | bytes 66052
  7.2 41.1 %all-gather.6.cloned.1.call-start = ((), (), s32[]{:S(2)}) async-start(), calls=%async_computation.7 | async-start | bytes 1966080 | tf_op jit(solution)/shard_map/all_gather | solution.py:276
  9.0 113.4 %all-gather.4.cloned.1.call-start = ((), (), s32[]{:S(2)}) async-start(), calls=%async_computation.5 | async-start | bytes 2129920 | tf_op jit(solution)/shard_map/all_gather | solution.py:275
  10.0 1.0 copy-start
  11.0 0.7 copy-start.3
  15.5 24.9 %all-to-all-start = ((bf16[64,16,128]{2,1,0:T(8,128)(2,1)}), bf16[64,16,128]{2,1,0:T(8,128)(2,1)S(1)}, u32[]{:S(2)}, u32[]{:S(2)}) async-start(bf16[64,16,128]{2,1,0:T(8,128)(2,1)} %bitcast), calls=%async_computation | async-start | bytes 524288 | tf_op jit(solution)/shard_map/all_to_all | solution.py:282
  40.4 7.8 %all-to-all-start.1 = ((bf16[4,48,128]{2,1,0:T(8,128)(2,1)}), bf16[4,48,128]{2,1,0:T(8,128)(2,1)S(1)}, u32[]{:S(2)}, u32[]{:S(2)}) async-start(bf16[4,48,128]{2,1,0:T(8,128)(2,1)} %pad.9), calls=%async_computation.1 | async-start | bytes 98304 | tf_op jit(solution)/shard_map/all_to_all | solution.py:281
  45.2 276.9 %all-reduce.5.cloned.1.call-start = ((), (), s32[]{:S(2)}) async-start(), calls=%async_computation.8 | async-start | bytes 524288
  48.3 74.1 %copy-start.6 = (bf16[4,48,128]{2,1,0:T(8,128)(2,1)}, bf16[4,48,128]{2,1,0:T(8,128)(2,1)S(1)}, u32[]{:S(2)}) copy-start(bf16[4,48,128]{2,1,0:T(8,128)(2,1)S(1)} %all-to-all-done.1.w_ref) | copy-start | bytes 147460
  148.7 320.6 %reduce-scatter.2.cloned.1.call-start = ((), (), s32[]{:S(2)}) async-start(), calls=%async_computation.6 | async-start | bytes 4259840 | tf_op jit(solution)/shard_map/reduce_scatter | solution.py:291
  152.7 0.9 copy-start.7
  153.6 24.5 %copy-start.11 = (u32[256]{0:T(256)S(1)}, u32[256]{0:T(256)}, u32[]{:S(2)}) copy-start(u32[256]{0:T(256)} %constant.23) | copy-start | bytes 3076
  173.3 162.6 %all-to-all-start.2 = ((bf16[4,48,4096]{2,1,0:T(8,128)(2,1)}), bf16[4,48,4096]{2,1,0:T(8,128)(2,1)S(1)}, u32[]{:S(2)}, u32[]{:S(2)}) async-start(bf16[4,48,4096]{2,1,0:T(8,128)(2,1)} %get-tuple-element.15), calls=%async_computation.2 | async-start | bytes 3145728 | tf_op jit(solution)/shard_map/all_to_all | solution.py:287
  323.5 11.8 %collective-permute-start = (f32[8,128]{1,0:T(8,128)S(1)}, f32[8,128]{1,0:T(8,128)S(1)}, u32[]{:S(2)}, u32[]{:S(2)}) collective-permute-start(f32[8,128]{1,0:T(8,128)S(1)} %dynamic-slice_bitcast_fusion), channel_id=1, source_target_pairs={{0,0},{1,64},{2,128},{3,192},{4,4},{5,68},{6,132},{7,196},{8,8},{9... | collective-permute-start | bytes 12296 | tf_op jit(solution)/shard_map/ppermute | solution.py:299
  335.9 133.4 %copy-start.1 = (f32[64,4096]{1,0:T(8,128)S(1)}, f32[64,4096]{1,0:T(8,128)}, u32[]{:S(2)}) copy-start(f32[64,4096]{1,0:T(8,128)} %get-tuple-element.17.own_ref) | copy-start | bytes 3145732
  335.9 133.4 %copy-start.4 = (s32[1,2]{1,0:T(1,128)S(1)}, s32[1,2]{1,0:T(1,128)}, u32[]{:S(2)}) copy-start(s32[1,2]{1,0:T(1,128)} %hub_ref.3) | copy-start | bytes 28
  335.9 1.2 copy-start.5
  469.3 0.8 copy-start.2
Sparse Core Ops, SparseCore 0:
  10.4 30.6 all-gather.5
  43.9 78.4 all-gather.3
  148.8 173.3 all-reduce.4
  326.7 142.5 reduce-scatter.1

commit v2 on v1

--- a/solution.py
+++ b/solution.py
@@ -35,41 +35,296 @@
     return (node == rows).astype(F32).astype(BF)
 
 
-def prep_kernel(hub_ref, hidden_ref, rows_ref, halo_ref, hubs_ref, total):
-    core = lax.rem(lax.axis_index("dom"), NC)
+def place():
+    dom = lax.axis_index("dom")
+    return dom // (NX * NC), lax.rem(dom // NC, NX), lax.rem(dom, NC), lax.axis_index("feat")
+
+
+def device(z, x, c, f):
+    return ((lax.rem(z, NZ) * NX + lax.rem(x, NX)) * NC + c, lax.rem(f, NF))
+
+
+def remote(src, dst, send, recv, target):
+    return pltpu.make_async_remote_copy(
+        src_ref=src,
+        dst_ref=dst,
+        send_sem=send,
+        recv_sem=recv,
+        device_id=target,
+        device_id_type=pl.DeviceIdType.MESH,
+    )
+
+
+def meet(targets):
+    barrier = pltpu.get_barrier_semaphore()
+    for target in targets:
+        pl.semaphore_signal(
+            barrier, inc=1, device_id=target, device_id_type=pl.DeviceIdType.MESH
+        )
+    return barrier
+
+
+HALF = ROWS_DEV // 2
+
+
+def gather_kernel(
+    hub_ref,
+    hidden_ref,
+    rows_ref,
+    gl_in,
+    ws_ref,
+    wn_ref,
+    gl_ref,
+    w_ref,
+    hubs_ref,
+    halo_ref,
+    wsend,
+    total,
+    outgoing,
+    sibling,
+    merged,
+    planes,
+    y_send,
+    y_recv,
+    w_send,
+    w_recv,
+    hx_send,
+    hx_recv,
+    hz_send,
+    hz_recv,
+    hc_send,
+    hc_recv,
+    c_send,
+    c_recv,
+    z_send,
+    z_recv,
+    x_send,
+    x_recv,
+):
+    z, x, c, f = place()
+    pair = device(z, x, 1 - c, f)
+    barrier = meet(
+        [device(z, x, c, f + o) for o in range(1, NF)]
+        + [device(z + o, x, c, f) for o in range(1, NZ)]
+        + [device(z, x + o, c, f) for o in range(1, NX)]
+        + [pair]
+    )
+
+    gl_ref[f, 32:GP, :] = jnp.zeros((GP - 32, ROWS_DEV), BF)
+    gl_ref[f, 0:GR, :] = gl_in[...]
+    for g in range(NF):
+        wsend[g] = jnp.zeros((GP, 2 * FD), BF)
+        cols = slice(g * FD, (g + 1) * FD)
+        wsend[g, 0:GR] = jnp.concatenate([ws_ref[:, cols], wn_ref[:, cols]], axis=1)
+    w_ref[f] = wsend[f]
     for i in range(HB):
-        start = pl.multiple_of(hub_ref[0, i] * BLK, BLK)
-        hubs_ref[i] = hidden_ref[:, pl.ds(start, BLK)]
+        wanted = hub_ref[0, i]
+        piece = hidden_ref[:, 0:BLK]
+        for b in range(1, NB):
+            piece = jnp.where(wanted == b, hidden_ref[:, b * BLK : (b + 1) * BLK], piece)
+        hubs_ref[z, x, c, i] = piece
+    pl.semaphore_wait(barrier, NF + NZ + NX - 2)
+
+    def y_copy(way, k, origin, half):
+        part = gl_ref.at[lax.rem(origin + NF, NF), :, pl.ds(half * HALF, HALF)]
+        target = device(z, x, c, f + (1 if way == 0 else NF - 1))
+        return remote(part, part, y_send.at[way, k], y_recv.at[way, k], target)
+
+    y_first = [y_copy(0, 0, f, 0), y_copy(1, 0, f, 1), y_copy(0, 1, f, 1), y_copy(1, 1, f, 0)]
+    for copy in y_first:
+        copy.start()
+
+    hx = [
+        remote(
+            hubs_ref.at[z, x, c],
+            hubs_ref.at[z, x, c],
+            hx_send.at[o - 1],
+            hx_recv.at[o - 1],
+            device(z, x + o, c, f),
+        )
+        for o in range(1, NX)
+    ]
+    for copy in hx:
+        copy.start()
+    ws = [
+        remote(
+            wsend.at[lax.rem(f + o, NF)],
+            w_ref.at[f],
+            w_send.at[o - 1],
+            w_recv.at[o - 1],
+            device(z, x, c, f + o),
+        )
+        for o in range(1, NF)
+    ]
+    for copy in ws:
+        copy.start()
+
+    def hz_copy(way, k, half):
+        origin = lax.rem(z + (NZ - k if way == 0 else k), NZ)
+        part = hubs_ref.at[origin, pl.ds(2 * half, 2), c]
+        target = device(z + (1 if way == 0 else NZ - 1), x, c, f)
+        return remote(part, part, hz_send.at[way, k, half], hz_recv.at[way, k, half], target)
+
+    def hc_copy(k, half):
+        part = hubs_ref.at[lax.rem(z + k, NZ), pl.ds(2 * half, 2), c]
+        return remote(part, part, hc_send.at[k, half], hc_recv.at[k, half], pair)
+
+    def hc_recv_wait(k, half):
+        part = hubs_ref.at[lax.rem(z + k, NZ), pl.ds(2 * half, 2), 1 - c]
+        remote(part, part, hc_send.at[k, half], hc_recv.at[k, half], pair).wait_recv()
+
+    def hz_wait(way, k, half):
+        origin = lax.rem(z + (NZ - k - 1 if way == 0 else k + 1), NZ)
+        part = hubs_ref.at[origin, pl.ds(2 * half, 2), c]
+        remote(part, part, hz_send.at[way, k, half], hz_recv.at[way, k, half], pair).wait_recv()
+
+    sent = []
+
+    def go(copy):
+        copy.start()
+        sent.append(copy)
+
     rows = rows_ref[...]
     total[...] = jnp.zeros_like(total)
 
-    @pl.loop(0, ROWS_DEV // CHUNK)
-    def _(i):
-        start = pl.multiple_of(i * CHUNK, CHUNK)
-        hot = one_hot_rows(rows, start, CHUNK)
-        total[...] += jnp.dot(hidden_ref[:, pl.ds(start, CHUNK)], hot, preferred_element_type=F32)
-
+    def gather(first, last):
+        @pl.loop(first, last)
+        def _(i):
+            start = pl.multiple_of(i * CHUNK, CHUNK)
+            hot = one_hot_rows(rows, start, CHUNK)
+            total[...] += jnp.dot(
+                hidden_ref[:, pl.ds(start, CHUNK)], hot, preferred_element_type=F32
+            )
+
+    gather(0, 3)
+    for o in range(1, NX):
+        part = hubs_ref.at[z, lax.rem(x + NX - o, NX), c]
+        remote(part, part, hx_send.at[o - 1], hx_recv.at[o - 1], pair).wait_recv()
+    for half in (0, 1):
+        go(hz_copy(0, 0, half))
+        go(hz_copy(1, 0, 1 - half))
+    for half in (0, 1):
+        go(hc_copy(0, half))
+    gather(3, ROWS_DEV // CHUNK)
     for k in range(NZ):
         piece = total[:, k * BLK : (k + 1) * BLK]
         zero = jnp.zeros_like(piece)
         both = jnp.concatenate(
-            [jnp.where(core == 0, piece, zero), jnp.where(core == 1, piece, zero)], axis=0
-        )
-        halo_ref[k] = both.T.astype(BF).reshape(NX, NC, CAP, BLK)
-
-
-def prep(hub_blocks, hidden, rows):
+            [jnp.where(c == 0, piece, zero), jnp.where(c == 1, piece, zero)], axis=0
+        )
+        outgoing[k] = both.T.astype(BF).reshape(NX, NC, CAP, BLK)
+    to_pair = remote(outgoing.at[:, :, 1 - c], sibling, c_send, c_recv, pair)
+    go(to_pair)
+
+    def y_wait(way, k, distance, half):
+        origin = lax.rem(f + (NF - distance if way == 0 else distance), NF)
+        part = gl_ref.at[origin, :, pl.ds(half * HALF, HALF)]
+        remote(part, part, y_send.at[way, k], y_recv.at[way, k], pair).wait_recv()
+
+    def ring(k):
+        for half in (0, 1):
+            for way in (0, 1):
+                part = half if way == 0 else 1 - half
+                if k == 3 and part != way:
+                    continue
+                hz_wait(way, k, part)
+                if k < 2 or (k == 2 and part == way):
+                    go(hz_copy(way, k + 1, part))
+                go(hc_copy(NZ - k - 1 if way == 0 else k + 1, part))
+
+    y_wait(0, 0, 1, 0)
+    go(y_copy(0, 2, f - 1, 0))
+    y_wait(1, 0, 1, 1)
+    go(y_copy(1, 2, f + 1, 1))
+    to_pair.wait_recv()
+    merged[...] = outgoing[:, :, c] + sibling[...]
+    for o in range(1, NZ):
+        go(
+            remote(
+                merged.at[lax.rem(z + o, NZ)],
+                planes.at[z],
+                z_send.at[o - 1],
+                z_recv.at[o - 1],
+                device(z + o, x, c, f),
+            )
+        )
+    planes[z] = merged[z]
+    ring(0)
+    for o in range(1, NZ):
+        part = planes.at[lax.rem(z + NZ - o, NZ)]
+        remote(part, part, z_send.at[o - 1], z_recv.at[o - 1], pair).wait_recv()
+    for o in range(1, NX):
+        go(
+            remote(
+                planes.at[:, lax.rem(x + o, NX)],
+                halo_ref.at[x],
+                x_send.at[o - 1],
+                x_recv.at[o - 1],
+                device(z, x + o, c, f),
+            )
+        )
+    halo_ref[x] = planes[:, x]
+    ring(1)
+    for o in range(1, NX):
+        part = halo_ref.at[lax.rem(x + NX - o, NX)]
+        remote(part, part, x_send.at[o - 1], x_recv.at[o - 1], pair).wait_recv()
+    ring(2)
+    ring(3)
+    for o in range(1, NF):
+        part = w_ref.at[lax.rem(f + NF - o, NF)]
+        remote(part, part, w_send.at[o - 1], w_recv.at[o - 1], pair).wait_recv()
+    y_wait(0, 1, 1, 1)
+    y_wait(1, 1, 1, 0)
+    y_wait(0, 2, 2, 0)
+    y_wait(1, 2, 2, 1)
+    for k in range(NZ):
+        for half in (0, 1):
+            hc_recv_wait(k, half)
+    for copy in y_first + hx + ws + sent:
+        copy.wait_send()
+
+
+def gather_all(hub_blocks, hidden, rows, grad_logits, weight_self, weight_neigh):
+    dma = pltpu.SemaphoreType.DMA
+    outs = (
+        jax.ShapeDtypeStruct((NF, GP, ROWS_DEV), BF),
+        jax.ShapeDtypeStruct((NF, GP, 2 * FD), BF),
+        jax.ShapeDtypeStruct((NZ, NX, NC, HB, FD, BLK), BF),
+        jax.ShapeDtypeStruct((NX, NZ, CAP, BLK), BF),
+    )
     return pl.pallas_call(
-        prep_kernel,
-        out_shape=(
-            jax.ShapeDtypeStruct((NZ, NX, NC, CAP, BLK), BF),
-            jax.ShapeDtypeStruct((HB, FD, BLK), BF),
+        gather_kernel,
+        out_shape=outs,
+        in_specs=[spec(pltpu.SMEM)] + [spec()] * 5,
+        out_specs=(spec(),) * 4,
+        scratch_shapes=[
+            VM((NF, GP, 2 * FD), BF),
+            VM((FD, PARTS * CAP), F32),
+            VM((NZ, NX, NC, CAP, BLK), BF),
+            VM((NZ, NX, CAP, BLK), BF),
+            VM((NZ, NX, CAP, BLK), BF),
+            VM((NZ, NX, CAP, BLK), BF),
+            dma((2, 3)),
+            dma((2, 3)),
+            dma((3,)),
+            dma((3,)),
+            dma((3,)),
+            dma((3,)),
+            dma((2, 4, 2)),
+            dma((2, 4, 2)),
+            dma((8, 2)),
+            dma((8, 2)),
+            dma,
+            dma,
+            dma((7,)),
+            dma((7,)),
+            dma((3,)),
+            dma((3,)),
+        ],
+        compiler_params=pltpu.CompilerParams(
+            collective_id=0, has_side_effects=True, vmem_limit_bytes=40 << 20
         ),
-        in_specs=[spec(pltpu.SMEM), spec(), spec()],
-        out_specs=(spec(), spec()),
-        scratch_shapes=[VM((FD, PARTS * CAP), F32)],
-        compiler_params=pltpu.CompilerParams(vmem_limit_bytes=32 << 20),
-    )(hub_blocks, hidden, rows)
+    )(hub_blocks, hidden, rows, grad_logits, weight_self, weight_neigh)
 
 
 def slot_place():
@@ -270,17 +525,10 @@
     grad_logits,
 ):
     rows = halo_rows.reshape(1, PARTS * CAP)
-    halo_out, hub_piece = prep(hub_blocks, hidden, rows)
-    pad = ((0, GP - GR), (0, 0))
-    hubs = lax.all_gather(hub_piece, "dom", axis=0, tiled=True)
-    gl = lax.all_gather(jnp.pad(grad_logits, pad), "feat", axis=0, tiled=False)
-    w = jnp.stack(
-        [weight_self.reshape(GR, NF, FD), weight_neigh.reshape(GR, NF, FD)], axis=2
-    ).reshape(GR, NF, 2 * FD)
-    w = jnp.pad(w.transpose(1, 0, 2), ((0, 0), (0, GP - GR), (0, 0)))
-    w = lax.all_to_all(w, "feat", 0, 0, tiled=True)
-    halo = lax.all_to_all(halo_out.reshape(PARTS, CAP, BLK), "dom", 0, 0, tiled=True)
-    halo = halo.reshape(NZ, NX, NC, CAP, BLK).sum(axis=2).transpose(1, 0, 2, 3)
+    gl, w, hubs, halo = gather_all(
+        hub_blocks, hidden, rows, grad_logits, weight_self, weight_neigh
+    )
+    hubs = hubs.reshape(PARTS * HB, FD, BLK)
     own, back, hubg, part, mine, pg = layer(
         tile_src, tiles, hidden, halo, hubs, halo_counts, gl, w
     )

time: 483 us -> 410 us (0.85)
  waiting for transfers between devices: 369 us -> 282 us
  Pallas kernels: 35.3 us -> 62.9 us
  starting transfers between devices: 26.5 us -> 9.95 us
    all_gather x2 -> x0, waiting for transfers between devices: 74.1 us -> none  [the longest x1 74.1 us: local(): hubs = lax.all_gather(hub_piece, 'dom', axis=0, tiled=True)]
    pallas_call x1, Pallas kernels: 3.84 us -> 31.4 us  [gather_all(): pl.pallas_call(gather_kernel, out_shape=outs, in_specs=[spec(pltpu.SMEM)]...]
    all_to_all x2 -> x0, starting transfers between devices: 16.7 us -> none  [the longest x1 11.9 us: local(): lax.all_to_all(halo_out.reshape(PARTS, CAP, BLK), 'dom', 0, 0, tiled=True)]
    all_to_all x2 -> x0, waiting for transfers between devices: 13.4 us -> none  [the longest x1 11 us: local(): lax.all_to_all(halo_out.reshape(PARTS, CAP, BLK), 'dom', 0, 0, tiled=True)]
    unnamed x27 -> x33, local copies, waits for them, and re-layouts: 6.33 us -> 13.2 us
    unnamed x5 -> x3, waiting for transfers between devices: 144 us -> 143 us
  transfers between devices with their start and end apart: 8 -> 4, of which waited for: 6 -> 3; matrix products, arithmetic and copies ran while one was open for 2% -> 2% of each run, Pallas kernels for 1% -> 0%
where the time goes in v2:
time: 410 us; the launch traced here: 409 us
  waiting for transfers between devices  282 us (69%)
  Pallas kernels  62.9 us (15%)
  blocking collectives  19.5 us (5%)
  local copies, waits for them, and re-layouts  15.3 us (4%)
  between operations  14.1 us (3%)
  starting transfers between devices  9.95 us (2%)
  other arithmetic  5.21 us (1%)
    unnamed x3, waiting for transfers between devices  143 us
    reduce_scatter x1, waiting for transfers between devices, local(): lax.psum_scatter(hubg.astype(F32), 'dom', scatter_dimension=0, tiled=True)  132 us
    pallas_call x1, Pallas kernels, gather_all(): pl.pallas_call(gather_kernel, out_shape=outs, in_specs=[spec(pltpu.SMEM)]...  31.4 us
    pallas_call x1, Pallas kernels, layer(): pl.pallas_call(layer_kernel, grid=(NB // 2,), out_shape=outs, in_specs=[s...  26.2 us
    all_to_all x1, blocking collectives, local(): lax.all_to_all(back.reshape(PARTS, CAP, BLK), 'dom', 0, 0, tiled=True)  19.5 us
    unnamed x33, local copies, waits for them, and re-layouts  13.2 us
  transfers between devices with their start and end apart: 4, of which 3 were waited for; matrix products, arithmetic and copies ran while one was open for 2% of the time, Pallas kernels for 0%

profile of v2, /device:TPU:16, one launch (start us, length us, event | category | flops | bytes accessed | tf_op | source)
XLA Modules:
  0.0 408.7 jit_solution(7844770073366336867)
XLA Ops:
  7.2 0.0 all-reduce.3.cloned.1.call-start
  7.2 1.4 copy.22.src_ref
  8.6 0.8 copy.21
  9.4 0.1 reshape.29.rows_ref
  9.5 1.0 copy-done
  10.5 1.0 copy-done.4
  11.5 0.7 copy-done.8
  12.2 0.7 copy-done.9
  13.0 0.7 copy-done.10
  13.6 31.4 %shard_map.120 = (bf16[4,48,4096]{2,1,0:T(8,128)(2,1)S(1)}, bf16[4,48,128]{2,1,0:T(8,128)(2,1)S(1)}, bf16[8,4,2,2,64,128]{5,4,3,2,1,0:T(8,128)(2,1)S(1)}, bf16[4,8,16,128]{3,2,1,0:T(8,128)(2,1)S(1)}) custom-call(s32[1,2]{1,0:T(1,128)S(1)} %copy-done.10, bf16[64,4096]{1,0:T(8,128)(2,1)S(1)} %copy-done, s32[1,1024]{1,0:T(1,128)S(1)} %reshape.29.rows_ref, ...), custom_call_target="tpu_custom_call" | custom-call | tf_op jit(solution)/shard_map/pallas_call | solution.py:295
  45.0 1.3 copy-done.1
  46.4 1.1 copy-done.2
  47.5 0.6 copy-done.5
  48.2 0.6 copy-done.7
  48.8 26.2 %shard_map.121 = (f32[64,4096]{1,0:T(8,128)}, bf16[4,8,16,128]{3,2,1,0:T(8,128)(2,1)}, bf16[128,64,128]{2,1,0:T(8,128)(2,1)}, bf16[4,48,4096]{2,1,0:T(8,128)(2,1...) custom-call(s32[32,12]{1,0:T(8,128)} %copy.22.src_ref, bf16[32,12,128,128]{3,2,1,0:T(8,128)(2,1)} %tiles_ref.1, ...), custom_call_target="tpu_custom_call" | custom-call | tf_op jit(solution)/shard_map/pallas_call | solution.py:461
  75.0 0.0 reduce-scatter.2.cloned.1.call-start
  75.1 4.0 convert_element_type.8
  79.1 0.9 copy-done.13
  80.1 19.5 %all_to_all.10 = bf16[64,16,128]{2,1,0:T(8,128)(2,1)S(1)} all-to-all(bf16[64,16,128]{2,1,0:T(8,128)(2,1)S(1)} %bitcast.22), channel_id=1, replica_groups=mesh['dom'=64,'feat'=4] {'dom'}, dimensions={0} | all-to-all | bytes 524288 | tf_op jit(solution)/shard_map/all_to_all | solution.py:550
  99.5 5.0 %all-to-all-start = ((bf16[4,48,4096]{2,1,0:T(8,128)(2,1)}), bf16[4,48,4096]{2,1,0:T(8,128)(2,1)S(1)}, u32[]{:S(2)}, u32[]{:S(2)}) async-start(bf16[4,48,4096]{2,1,0:T(8,128)(2,1)} %get-tuple-element.19), calls=%async_computation | async-start | bytes 3145728 | tf_op jit(solution)/shard_map/all_to_all | solution.py:535
  104.6 0.6 dynamic-slice
  105.2 143.2 %all-reduce.3.cloned.1.call-done = f32[64,8,128]{2,1,0:T(8,128)} async-done(((f32[64,8,128]{2,1,0:T(8,128)}), f32[64,8,128]{2,1,0:T(8,128)}) %all-reduce.3.cloned.1.call-update) | async-done | bytes 262160
  248.4 1.3 dynamic-slice_bitcast_fusion
  249.7 4.8 %collective-permute-start = (f32[8,128]{1,0:T(8,128)S(1)}, f32[8,128]{1,0:T(8,128)S(1)}, u32[]{:S(2)}, u32[]{:S(2)}) collective-permute-start(f32[8,128]{1,0:T(8,128)S(1)} %dynamic-slice_bitcast_fusion), channel_id=1, source_target_pairs={{0,0},{1,64},{2,128},{3,192},{4,4},{5,68},{6,132},{7,196},{8,8},{9... | collective-permute-start | bytes 12296 | tf_op jit(solution)/shard_map/ppermute | solution.py:547
  254.6 7.0 %collective-permute-done = f32[8,128]{1,0:T(8,128)S(1)} collective-permute-done((f32[8,128]{1,0:T(8,128)S(1)}, f32[8,128]{1,0:T(8,128)S(1)}, u32[]{:S(2)}, u32[]{:S(2)}) %collective-permute-start) | collective-permute-done | bytes 4128 | tf_op jit(solution)/shard_map/ppermute | solution.py:547
  261.5 0.6 slice_bitcast_fusion.2
  262.2 0.4 select_reduce_fusion
  262.6 0.8 copy-done.12
  263.4 0.8 fusion
  264.2 131.5 %reduce-scatter.2.cloned.1.call-done.sum_ref = f32[2,64,128]{2,1,0:T(8,128)} async-done(((f32[128,64,128]{2,1,0:T(8,128)}), f32[2,64,128]{2,1,0:T(8,128)}) %reduce-scatter.2.cloned.1.call-update) | async-done | bytes 65552 | tf_op jit(solution)/shard_map/reduce_scatter | solution.py:539
  395.8 0.8 copy-done.6
  396.6 5.2 %shard_map.122 = f32[64,4096]{1,0:T(8,128)} custom-call(s32[1,2]{1,0:T(1,128)S(1)} %copy-done.11, f32[64,4096]{1,0:T(8,128)S(1)} %copy-done.3, s32[1,1024]{1,0:T(1,128)S(1)} %reshape.29.rows_ref, bf16[32,16,128]{2,1,0:T(8,128)(2,1)S(1)} %get-tuple-element.25.first_ref, bf16[32,16,128]{2,1,0:T(8,128)(2,1)S(1)} %get-tuple-element.24.second_ref, ...), custom_call_target="tpu_custom_call" | custom-call | tf_op jit(solution)/shard_map/pallas_call | solution.py:507
  (25 shorter events, 0.1 us)
Async XLA Ops:
  7.2 241.3 %all-reduce.3.cloned.1.call-start = ((), (), s32[]{:S(2)}) async-start(), calls=%async_computation.4 | async-start | bytes 524288
  9.5 1.0 copy-start
  10.5 1.0 copy-start.4
  11.5 0.7 copy-start.8
  12.2 0.7 copy-start.9
  13.0 0.7 copy-start.10
  45.0 1.3 copy-start.1
  46.4 1.1 copy-start.2
  47.5 0.6 copy-start.5
  48.2 0.6 copy-start.7
  75.0 320.7 %reduce-scatter.2.cloned.1.call-start = ((), (), s32[]{:S(2)}) async-start(), calls=%async_computation.3 | async-start | bytes 4259840 | tf_op jit(solution)/shard_map/reduce_scatter | solution.py:539
  79.1 0.9 copy-start.13
  80.0 24.6 %copy-start.14 = (u32[256]{0:T(256)S(1)}, u32[256]{0:T(256)}, u32[]{:S(2)}) copy-start(u32[256]{0:T(256)} %constant.15) | copy-start | bytes 3076
  99.5 162.6 %all-to-all-start = ((bf16[4,48,4096]{2,1,0:T(8,128)(2,1)}), bf16[4,48,4096]{2,1,0:T(8,128)(2,1)S(1)}, u32[]{:S(2)}, u32[]{:S(2)}) async-start(bf16[4,48,4096]{2,1,0:T(8,128)(2,1)} %get-tuple-element.19), calls=%async_computation | async-start | bytes 3145728 | tf_op jit(solution)/shard_map/all_to_all | solution.py:535
  249.7 11.8 %collective-permute-start = (f32[8,128]{1,0:T(8,128)S(1)}, f32[8,128]{1,0:T(8,128)S(1)}, u32[]{:S(2)}, u32[]{:S(2)}) collective-permute-start(f32[8,128]{1,0:T(8,128)S(1)} %dynamic-slice_bitcast_fusion), channel_id=1, source_target_pairs={{0,0},{1,64},{2,128},{3,192},{4,4},{5,68},{6,132},{7,196},{8,8},{9... | collective-permute-start | bytes 12296 | tf_op jit(solution)/shard_map/ppermute | solution.py:547
  262.2 133.6 %copy-start.3 = (f32[64,4096]{1,0:T(8,128)S(1)}, f32[64,4096]{1,0:T(8,128)}, u32[]{:S(2)}) copy-start(f32[64,4096]{1,0:T(8,128)} %get-tuple-element.21.own_ref) | copy-start | bytes 3145732
  262.2 133.6 %copy-start.11 = (s32[1,2]{1,0:T(1,128)S(1)}, s32[1,2]{1,0:T(1,128)}, u32[]{:S(2)}) copy-start(s32[1,2]{1,0:T(1,128)} %hub_ref.3) | copy-start | bytes 28
  262.2 1.2 copy-start.12
  395.8 0.8 copy-start.6
Sparse Core Ops, SparseCore 0:
  75.2 173.2 all-reduce.2
  253.1 142.6 reduce-scatter.1

commit v3 on v2

--- a/solution.py
+++ b/solution.py
@@ -480,37 +480,366 @@
     )(src, tiles, hidden, halo, hubs, counts, gl, w)
 
 
-def finish_kernel(hub_ref, own_ref, rows_ref, first_ref, second_ref, sum_ref, out_ref):
-    core = lax.rem(lax.axis_index("dom"), NC)
+def return_kernel(
+    hub_ref,
+    rows_ref,
+    own_ref,
+    back_ref,
+    hubg_ref,
+    part_ref,
+    mine_ref,
+    pg_ref,
+    logits_ref,
+    gself_ref,
+    gneigh_ref,
+    out_ref,
+    y_mid,
+    y_stage,
+    y_last,
+    pairs,
+    arrive,
+    stage,
+    x_stage,
+    x_got,
+    xsum,
+    k_first,
+    k_mine,
+    k_pair,
+    g_pair,
+    g_sum,
+    g_x,
+    g_row,
+    g_z,
+    g_last,
+    g_final,
+    y_send,
+    y_recv,
+    pc_send,
+    pc_recv,
+    r_send,
+    r_recv,
+    rx_send,
+    rx_recv,
+    kx_send,
+    kx_recv,
+    kz_send,
+    kz_recv,
+    kc_send,
+    kc_recv,
+    gc_send,
+    gc_recv,
+    gx_send,
+    gx_recv,
+    gz_send,
+    gz_recv,
+    gm_send,
+    gm_recv,
+):
+    z, x, c, f = place()
+    pair = device(z, x, 1 - c, f)
+    group = z // 2
+    swap = device(2 * f + lax.rem(z, 2), x, c, group)
+    barrier = meet(
+        [device(z, x, c, f + o) for o in (1, NF - 1)]
+        + [device(z + o, x, c, f) for o in range(1, NZ)]
+        + [device(z, x + o, c, f) for o in range(1, NX)]
+        + [pair]
+    )
+
+    @pl.when(f != group)
+    def _():
+        meet([swap])
+
+    pl.semaphore_wait(barrier, jnp.where(f != group, 2 + NZ + NX, 1 + NZ + NX))
+    sent = []
+
+    def go(copy):
+        copy.start()
+        sent.append(copy)
+        return copy
+
+    def y_cols(half):
+        return pl.ds(half * HALF, HALF)
+
+    def y_copy(way, k, src, dst):
+        target = device(z, x, c, f + (1 if way == 0 else NF - 1))
+        return remote(src, dst, y_send.at[way, k], y_recv.at[way, k], target)
+
+    def y_part(distance, half):
+        return part_ref.at[lax.rem(f + distance, NF), :, y_cols(half)]
+
+    y0 = [go(y_copy(w, 0, y_part(2, w), y_mid.at[w])) for w in (0, 1)]
+    y1 = [
+        go(y_copy(w, 1, y_part(1 if w == 0 else NF - 1, 1 - w), y_last.at[w, 1 - w]))
+        for w in (0, 1)
+    ]
+
+    order = (4, 3, 5, 2, 6, 1, 7, 0)
+    to_pair = {}
+    for o in order:
+        dest = lax.rem(z + o, NZ)
+        to_pair[o] = go(
+            remote(hubg_ref.at[dest, :, 1 - c], pairs.at[dest], pc_send.at[o], pc_recv.at[o], pair)
+        )
+    g_to_pair = go(remote(pg_ref.at[:, :, 1 - c], g_pair, gc_send, gc_recv, pair))
+    kx = [
+        go(
+            remote(
+                back_ref.at[lax.rem(x + o, NX)],
+                k_first.at[x],
+                kx_send.at[o - 1],
+                kx_recv.at[o - 1],
+                device(z, x + o, c, f),
+            )
+        )
+        for o in range(1, NX)
+    ]
+    k_first[x] = back_ref[x]
+
+    ring = {}
+
+    def hub_step(k):
+        distance = NZ // 2 - k
+        for o in {distance, NZ - distance}:
+            to_pair[o].wait_recv()
+        for half in (0, 1):
+            for way in (0, 1):
+                h = half if way == 0 else 1 - half
+                if k == 0 and h != way:
+                    continue
+                dest = lax.rem(z + (distance if way == 0 else NZ - distance), NZ)
+                xs = slice(2 * h, 2 * h + 2)
+                value = hubg_ref[dest, xs, c].astype(F32) + pairs[dest, xs].astype(F32)
+                if k > 1 or (k == 1 and h == way):
+                    ring[way, k - 1, h].wait_recv()
+                    value = value + arrive[way, k - 1, h].astype(F32)
+                stage[way, k, h] = value.astype(BF)
+                ring[way, k, h] = go(
+                    remote(
+                        stage.at[way, k, h],
+                        arrive.at[way, k, h],
+                        r_send.at[way, k, h],
+                        r_recv.at[way, k, h],
+                        device(z + (1 if way == 0 else NZ - 1), x, c, f),
+                    )
+                )
+
+    hub_step(0)
+    for copy in kx:
+        copy.wait_recv()
+    kz = [
+        go(
+            remote(
+                k_first.at[:, lax.rem(z + o, NZ)],
+                k_mine.at[z],
+                kz_send.at[o - 1],
+                kz_recv.at[o - 1],
+                device(z + o, x, c, f),
+            )
+        )
+        for o in range(1, NZ)
+    ]
+    k_mine[z] = k_first[:, z]
+    hub_step(1)
+
+    y2 = []
+    for w in (0, 1):
+        y0[w].wait_recv()
+        near = lax.rem(f + (1 if w == 0 else NF - 1), NF)
+        value = part_ref[near, :, y_cols(w)].astype(F32) + y_mid[w].astype(F32)
+        y_stage[w] = value.astype(BF)
+        y2.append(go(y_copy(w, 2, y_stage.at[w], y_last.at[w, w])))
+
+    for copy in kz:
+        copy.wait_recv()
+    kc = go(remote(k_mine, k_pair, kc_send, kc_recv, pair))
+    hub_step(2)
+
+    g_to_pair.wait_recv()
+    g_sum[...] = pg_ref[:, :, c] + g_pair[...]
+    gx = [
+        go(
+            remote(
+                g_sum.at[:, lax.rem(x + o, NX)],
+                g_x.at[o - 1],
+                gx_send.at[o - 1],
+                gx_recv.at[o - 1],
+                device(z, x + o, c, f),
+            )
+        )
+        for o in range(1, NX)
+    ]
+
+    kc.wait_recv()
     flat = []
-    for k in range(NZ * NX // 4):
-        a = first_ref[pl.ds(4 * k, 4)]
-        b = second_ref[pl.ds(4 * k, 4)]
-        turned = jnp.stack([a, b], axis=1).reshape(BLK, BLK).astype(F32).T
-        flat.append(jnp.where(core == 0, turned[0:FD], turned[FD:]).astype(BF))
+    for k in range(NZ):
+        a, b = k_mine[k], k_pair[k]
+        first = jnp.where(c == 0, a, b)
+        second = jnp.where(c == 0, b, a)
+        turned = jnp.stack([first, second], axis=1).reshape(BLK, BLK).astype(F32).T
+        flat.append(jnp.where(c == 0, turned[0:FD], turned[FD:]).astype(BF))
     back = jnp.concatenate(flat, axis=1)
     rows = rows_ref[...]
 
-    @pl.loop(0, ROWS_DEV // CHUNK)
-    def _(i):
-        start = pl.multiple_of(i * CHUNK, CHUNK)
-        hot = one_hot_rows(rows, start, CHUNK)
-        got = lax.dot_general(back, hot, NT, preferred_element_type=F32)
-        out_ref[:, pl.ds(start, CHUNK)] = own_ref[:, pl.ds(start, CHUNK)] + got
-
-    for i in range(HB):
-        start = pl.multiple_of(hub_ref[0, i] * BLK, BLK)
-        out_ref[:, pl.ds(start, BLK)] += sum_ref[i]
-
-
-def finish(hub_blocks, own, rows, first, second, hub_sum):
+    def scatter(first, last):
+        @pl.loop(first, last)
+        def _(i):
+            start = pl.multiple_of(i * CHUNK, CHUNK)
+            hot = one_hot_rows(rows, start, CHUNK)
+            got = lax.dot_general(back, hot, NT, preferred_element_type=F32)
+            out_ref[:, pl.ds(start, CHUNK)] = own_ref[:, pl.ds(start, CHUNK)] + got
+
+    scatter(0, 3)
+    hub_step(3)
+    for copy in gx:
+        copy.wait_recv()
+    g_row[...] = g_sum[:, x] + g_x[0] + g_x[1] + g_x[2]
+    gz = [
+        go(
+            remote(
+                g_row.at[lax.rem(z + o, NZ)],
+                g_z.at[o - 1],
+                gz_send.at[o - 1],
+                gz_recv.at[o - 1],
+                device(z + o, x, c, f),
+            )
+        )
+        for o in range(1, NZ)
+    ]
+    scatter(3, ROWS_DEV // CHUNK)
+
+    for copy in gz:
+        copy.wait_recv()
+    done = g_row[z]
+    for o in range(1, NZ):
+        done = done + g_z[o - 1]
+    g_last[...] = done
+    move = remote(g_last, g_final, gm_send, gm_recv, swap)
+
+    @pl.when(f != group)
+    def _():
+        move.start()
+
+    @pl.when(f == group)
+    def _():
+        g_final[...] = done
+
+    for half in (0, 1):
+        xs = slice(2 * half, 2 * half + 2)
+        value = hubg_ref[z, xs, c].astype(F32)
+        if half == 0:
+            to_pair[0].wait_recv()
+        value = value + pairs[z, xs].astype(F32)
+        for way in (0, 1):
+            ring[way, 3, half].wait_recv()
+            value = value + arrive[way, 3, half].astype(F32)
+        xsum[xs] = value
+    x_stage[...] = xsum[...].astype(BF)
+    hx = [
+        go(
+            remote(
+                x_stage.at[lax.rem(x + o, NX)],
+                x_got.at[o - 1],
+                rx_send.at[o - 1],
+                rx_recv.at[o - 1],
+                device(z, x + o, c, f),
+            )
+        )
+        for o in range(1, NX)
+    ]
+
+    for copy in y1 + y2:
+        copy.wait_recv()
+    for half in (0, 1):
+        cols = y_cols(half)
+        value = mine_ref[0:GR, cols]
+        for w in (0, 1):
+            value = value + y_last[w, half, 0:GR].astype(F32)
+        logits_ref[:, cols] = value.astype(BF)
+
+    for copy in hx:
+        copy.wait_recv()
+    total = xsum[x]
+    for o in range(1, NX):
+        total = total + x_got[o - 1].astype(F32)
+    for b in range(NB):
+        cols = slice(b * BLK, (b + 1) * BLK)
+        value = out_ref[:, cols]
+        for i in range(HB):
+            value = jnp.where(hub_ref[0, i] == b, value + total[i], value)
+        out_ref[:, cols] = value
+
+    @pl.when(f != group)
+    def _():
+        move.wait()
+
+    turned = jnp.concatenate([g_final[...], jnp.zeros((BLK - 8, BLK), F32)], axis=0).T
+    gself_ref[...] = turned[0:GR, 0:4]
+    gneigh_ref[...] = turned[0:GR, 4:8]
+    for copy in sent:
+        copy.wait_send()
+
+
+def return_all(hub_blocks, rows, own, back, hubg, part, mine, pg):
+    dma = pltpu.SemaphoreType.DMA
+    outs = (
+        jax.ShapeDtypeStruct((GR, ROWS_DEV), BF),
+        jax.ShapeDtypeStruct((GR, 4), F32),
+        jax.ShapeDtypeStruct((GR, 4), F32),
+        jax.ShapeDtypeStruct((FD, ROWS_DEV), F32),
+    )
     return pl.pallas_call(
-        finish_kernel,
-        out_shape=jax.ShapeDtypeStruct((FD, ROWS_DEV), F32),
-        in_specs=[spec(pltpu.SMEM)] + [spec()] * 5,
-        out_specs=spec(),
-        compiler_params=pltpu.CompilerParams(vmem_limit_bytes=32 << 20),
-    )(hub_blocks, own, rows, first, second, hub_sum)
+        return_kernel,
+        out_shape=outs,
+        in_specs=[spec(pltpu.SMEM)] + [spec()] * 7,
+        out_specs=(spec(),) * 4,
+        scratch_shapes=[
+            VM((2, GP, HALF), BF),
+            VM((2, GP, HALF), BF),
+            VM((2, 2, GP, HALF), BF),
+            VM((NZ, NX, HB, FD, BLK), BF),
+            VM((2, 4, 2, 2, HB, FD, BLK), BF),
+            VM((2, 4, 2, 2, HB, FD, BLK), BF),
+            VM((NX, HB, FD, BLK), BF),
+            VM((NX - 1, HB, FD, BLK), BF),
+            VM((NX, HB, FD, BLK), F32),
+            VM((NX, NZ, CAP, BLK), BF),
+            VM((NZ, NX, CAP, BLK), BF),
+            VM((NZ, NX, CAP, BLK), BF),
+            VM((NZ, NX, 8, BLK), F32),
+            VM((NZ, NX, 8, BLK), F32),
+            VM((NX - 1, NZ, 8, BLK), F32),
+            VM((NZ, 8, BLK), F32),
+            VM((NZ - 1, 8, BLK), F32),
+            VM((8, BLK), F32),
+            VM((8, BLK), F32),
+            dma((2, 3)),
+            dma((2, 3)),
+            dma((8,)),
+            dma((8,)),
+            dma((2, 4, 2)),
+            dma((2, 4, 2)),
+            dma((3,)),
+            dma((3,)),
+            dma((3,)),
+            dma((3,)),
+            dma((7,)),
+            dma((7,)),
+            dma,
+            dma,
+            dma,
+            dma,
+            dma((3,)),
+            dma((3,)),
+            dma((7,)),
+            dma((7,)),
+            dma,
+            dma,
+        ],
+        compiler_params=pltpu.CompilerParams(
+            collective_id=1, has_side_effects=True, vmem_limit_bytes=48 << 20
+        ),
+    )(hub_blocks, rows, own, back, hubg, part, mine, pg)
 
 
 def local(
@@ -532,25 +861,9 @@
     own, back, hubg, part, mine, pg = layer(
         tile_src, tiles, hidden, halo, hubs, halo_counts, gl, w
     )
-    parts = lax.all_to_all(part, "feat", 0, 0, tiled=True)
-    feat = lax.axis_index("feat")
-    others = jnp.arange(NF)[:, None, None] != feat
-    logits = (mine + jnp.where(others, parts.astype(F32), 0.0).sum(axis=0))[:GR].astype(BF)
-    hub_sum = lax.psum_scatter(hubg.astype(F32), "dom", scatter_dimension=0, tiled=True)
-    pg = lax.psum_scatter(pg.reshape(PARTS, 8, BLK), "dom", scatter_dimension=0, tiled=True)[0]
-    moves = [
-        ((16 * g + j) * NF + f, (16 * f + j) * NF + g)
-        for g in range(NF)
-        for j in range(16)
-        for f in range(NF)
-    ]
-    pg = lax.ppermute(pg, ("dom", "feat"), moves)
-    grad_self, grad_neigh = pg[:4, :GR].T, pg[4:, :GR].T
-    back = jnp.broadcast_to(back.transpose(1, 0, 2, 3)[:, :, None], (NZ, NX, NC, CAP, BLK))
-    back = lax.all_to_all(back.reshape(PARTS, CAP, BLK), "dom", 0, 0, tiled=True)
-    back = back.reshape(NZ * NX, NC, CAP, BLK)
-    grad_hidden = finish(hub_blocks, own, rows, back[:, 0], back[:, 1], hub_sum)
-    return logits, grad_self, grad_neigh, grad_hidden
+    hubg = hubg.reshape(NZ, NX, NC, HB, FD, BLK)
+    pg = pg.reshape(NZ, NX, NC, 8, BLK)
+    return return_all(hub_blocks, rows, own, back, hubg, part, mine, pg)
 
 
 def solution(mesh):

time: 410 us -> 113 us (0.28)
  waiting for transfers between devices: 282 us -> 0 us
  Pallas kernels: 62.9 us -> 92 us
  blocking collectives: 19.5 us -> 0 us
  between operations: 14.1 us -> 0.68 us
  starting transfers between devices: 9.95 us -> 0 us
  other arithmetic: 5.21 us -> 0 us
    unnamed x3 -> x0, waiting for transfers between devices: 143 us -> none
    reduce_scatter x1 -> x0, waiting for transfers between devices: 132 us -> none  [local(): lax.psum_scatter(hubg.astype(F32), 'dom', scatter_dimension=0, tiled=True)]
    pallas_call x1, Pallas kernels: 5.23 us -> 34.5 us  [return_all(): pl.pallas_call(return_kernel, out_shape=outs, in_specs=[spec(pltpu.SMEM)]...]
    all_to_all x1 -> x0, blocking collectives: 19.5 us -> none  [local(): lax.all_to_all(back.reshape(PARTS, CAP, BLK), 'dom', 0, 0, tiled=True)]
    ppermute x1 -> x0, waiting for transfers between devices: 6.95 us -> none  [local(): pg = lax.ppermute(pg, ('dom', 'feat'), moves)]
    all_to_all x1 -> x0, starting transfers between devices: 5.05 us -> none  [local(): parts = lax.all_to_all(part, 'feat', 0, 0, tiled=True)]
    ppermute x1 -> x0, starting transfers between devices: 4.82 us -> none  [local(): pg = lax.ppermute(pg, ('dom', 'feat'), moves)]
    unnamed x33 -> x34, local copies, waits for them, and re-layouts: 13.2 us -> 17.5 us
  transfers between devices with their start and end apart: 4 -> 0, of which waited for: 3 -> 0; matrix products, arithmetic and copies ran while one was open for 2% -> 0% of each run, Pallas kernels for 0% -> 0%
where the time goes in v3:
time: 113 us; the launch traced here: 112 us
  Pallas kernels  92 us (81%)
  local copies, waits for them, and re-layouts  18.8 us (17%)
    pallas_call x1, Pallas kernels, return_all(): pl.pallas_call(return_kernel, out_shape=outs, in_specs=[spec(pltpu.SMEM)]...  34.5 us
    pallas_call x1, Pallas kernels, gather_all(): pl.pallas_call(gather_kernel, out_shape=outs, in_specs=[spec(pltpu.SMEM)]...  31.4 us
    pallas_call x1, Pallas kernels, layer(): pl.pallas_call(layer_kernel, grid=(NB // 2,), out_shape=outs, in_specs=[s...  26.2 us
    unnamed x34, local copies, waits for them, and re-layouts  17.5 us

profile of v3, /device:TPU:16, one launch (start us, length us, event | category | flops | bytes accessed | tf_op | source)
XLA Modules:
  0.0 111.6 jit_solution(14887347362922976379)
XLA Ops:
  0.6 1.4 %copy.18.src_ref = s32[32,12]{1,0:T(8,128)} copy(s32[32,12]{0,1:T(8,128)} %param.11) | data formatting | bytes 3072 | tf_op args[2]
  2.0 0.8 copy.17
  2.8 0.1 reshape.20.rows_ref
  2.9 0.0 copy-start
  2.9 1.0 copy-done
  3.9 0.0 copy-start.6
  3.9 1.0 copy-done.6
  4.9 0.0 copy-start.11
  4.9 0.7 copy-done.11
  5.7 0.0 copy-start.12
  5.7 0.7 copy-done.12
  6.4 0.0 copy-start.13
  6.4 0.7 copy-done.13
  7.0 31.4 %shard_map.120 = (bf16[4,48,4096]{2,1,0:T(8,128)(2,1)S(1)}, bf16[4,48,128]{2,1,0:T(8,128)(2,1)S(1)}, bf16[8,4,2,2,64,128]{5,4,3,2,1,0:T(8,128)(2,1)S(1)}, bf16[4,8,16,128]{3,2,1,0:T(8,128)(2,1)S(1)}) custom-call(s32[1,2]{1,0:T(1,128)S(1)} %copy-done.13, bf16[64,4096]{1,0:T(8,128)(2,1)S(1)} %copy-done, s32[1,1024]{1,0:T(1,128)S(1)} %reshape.20.rows_ref, ...), custom_call_target="tpu_custom_call" | custom-call | tf_op jit(solution)/shard_map/pallas_call | solution.py:295
  38.4 0.0 copy-start.1
  38.5 1.3 %copy-done.1 = bf16[8,4,2,2,64,128]{5,4,3,2,1,0:T(8,128)(2,1)} copy-done((bf16[8,4,2,2,64,128]{5,4,3,2,1,0:T(8,128)(2,1)}, bf16[8,4,2,2,64,128]{5,4,3,2,1,0:T(8,128)(2,1)S(1)}, u32[]{:S(2)}) %copy-start.1) | copy-done | bytes 2097176
  39.8 0.0 copy-start.2
  39.8 1.2 %copy-done.2 = bf16[4,48,4096]{2,1,0:T(8,128)(2,1)} copy-done((bf16[4,48,4096]{2,1,0:T(8,128)(2,1)}, bf16[4,48,4096]{2,1,0:T(8,128)(2,1)S(1)}, u32[]{:S(2)}) %copy-start.2) | copy-done | bytes 1572888
  41.0 0.6 copy-done.8
  41.6 0.6 copy-done.10
  42.3 26.2 %shard_map.121 = (f32[64,4096]{1,0:T(8,128)}, bf16[4,8,16,128]{3,2,1,0:T(8,128)(2,1)}, bf16[128,64,128]{2,1,0:T(8,128)(2,1)}, bf16[4,48,4096]{2,1,0:T(8,128)(2,1...) custom-call(s32[32,12]{1,0:T(8,128)} %copy.18.src_ref, bf16[32,12,128,128]{3,2,1,0:T(8,128)(2,1)} %tiles_ref.1, ...), custom_call_target="tpu_custom_call" | custom-call | tf_op jit(solution)/shard_map/pallas_call | solution.py:461
  68.4 0.0 copy-done.14
  68.4 1.4 %copy-done.3 = bf16[4,48,4096]{2,1,0:T(8,128)(2,1)S(1)} copy-done((bf16[4,48,4096]{2,1,0:T(8,128)(2,1)S(1)}, bf16[4,48,4096]{2,1,0:T(8,128)(2,1)}, u32[]{:S(2)}) %copy-start.3) | copy-done | bytes 1572888
  69.8 1.2 %copy-done.4 = f32[64,4096]{1,0:T(8,128)S(1)} copy-done((f32[64,4096]{1,0:T(8,128)S(1)}, f32[64,4096]{1,0:T(8,128)}, u32[]{:S(2)}) %copy-start.4) | copy-done | bytes 1048600
  71.1 1.1 %copy-done.5 = f32[48,4096]{1,0:T(8,128)S(1)} copy-done((f32[48,4096]{1,0:T(8,128)S(1)}, f32[48,4096]{1,0:T(8,128)}, u32[]{:S(2)}) %copy-start.5) | copy-done | bytes 786456
  72.2 0.9 copy-done.7
  73.1 0.9 copy-done.9
  74.0 34.5 %shard_map.122 = (bf16[43,4096]{1,0:T(8,128)(2,1)S(1)}, f32[43,4]{1,0:T(8,128)S(1)}, f32[43,4]{1,0:T(8,128)S(1)}, f32[64,4096]{1,0:T(8,128)S(1)}) custom-call(s32[1,2]{1,0:T(1,128)S(1)} %copy-done.14, s32[1,1024]{1,0:T(1,128)S(1)} %reshape.20.rows_ref, f32[64,4096]{1,0:T(8,128)S(1)} %copy-done.4, bf16[4,8,16,128]{3,2,1,0:T(8,128)(2,1)S(1)} %copy-done.9, ...), custom_call_target="tpu_custom_call" | custom-call | tf_op jit(solution)/shard_map/pallas_call | solution.py:791
  108.5 0.7 copy.19
  109.2 0.7 copy.20
  109.9 0.7 copy.23
  110.6 1.0 copy.24
  (8 shorter events, 0.0 us)
Async XLA Ops:
  2.9 1.0 copy-start
  3.9 1.0 copy-start.6
  4.9 0.7 copy-start.11
  5.7 0.7 copy-start.12
  6.4 0.7 copy-start.13
  38.4 1.3 %copy-start.1 = (bf16[8,4,2,2,64,128]{5,4,3,2,1,0:T(8,128)(2,1)}, bf16[8,4,2,2,64,128]{5,4,3,2,1,0:T(8,128)(2,1)S(1)}, u32[]{:S(2)}) copy-start(bf16[8,4,2,2,64,128]{5,4,3,2,1,0:T(8,128)(2,1)S(1)} %get-tuple-element.15) | copy-start | bytes 6291460
  39.8 1.2 %copy-start.2 = (bf16[4,48,4096]{2,1,0:T(8,128)(2,1)}, bf16[4,48,4096]{2,1,0:T(8,128)(2,1)S(1)}, u32[]{:S(2)}) copy-start(bf16[4,48,4096]{2,1,0:T(8,128)(2,1)S(1)} %get-tuple-element.16.gl_ref) | copy-start | bytes 4718596
  41.0 0.7 copy-start.8
  41.6 0.6 copy-start.10
  42.3 26.2 %copy-start.14 = (s32[1,2]{1,0:T(1,128)S(1)}, s32[1,2]{1,0:T(1,128)}, u32[]{:S(2)}) copy-start(s32[1,2]{1,0:T(1,128)} %hub_ref.3) | copy-start | bytes 28
  68.4 1.4 %copy-start.3 = (bf16[4,48,4096]{2,1,0:T(8,128)(2,1)S(1)}, bf16[4,48,4096]{2,1,0:T(8,128)(2,1)}, u32[]{:S(2)}) copy-start(bf16[4,48,4096]{2,1,0:T(8,128)(2,1)} %get-tuple-element.21.part_ref) | copy-start | bytes 4718596
  69.8 1.2 %copy-start.4 = (f32[64,4096]{1,0:T(8,128)S(1)}, f32[64,4096]{1,0:T(8,128)}, u32[]{:S(2)}) copy-start(f32[64,4096]{1,0:T(8,128)} %get-tuple-element.18.own_ref) | copy-start | bytes 3145732
  71.1 1.1 %copy-start.5 = (f32[48,4096]{1,0:T(8,128)S(1)}, f32[48,4096]{1,0:T(8,128)}, u32[]{:S(2)}) copy-start(f32[48,4096]{1,0:T(8,128)} %get-tuple-element.22.mine_ref) | copy-start | bytes 2359300
  72.2 0.9 copy-start.7
  73.1 0.9 copy-start.9

commit v4 on v0

v4 whole, which is shorter than its diff:
```python
import jax
import jax.numpy as jnp
from jax import lax
from jax.experimental import pallas as pl
from jax.experimental.pallas import tpu as pltpu
from jax.sharding import PartitionSpec as P

BF = jnp.bfloat16
F32 = jnp.float32
BLK = 128
ROWS_DEV = 4096
TPB = 12
HB = 2
CAP = 16
NB = 32
NZ, NX, NC, NF = 8, 4, 2, 4
PARTS = NZ * NX * NC
GR = 43
GP = 48
FD = 64
EXT = 168
TR = 80
VM = pltpu.VMEM
CHUNK = 512
NT = (((1,), (1,)), ((), ()))
TN = (((0,), (0,)), ((), ()))


def spec(space=pltpu.VMEM):
    return pl.BlockSpec(memory_space=space)


def one_hot_rows(rows, start, size):
    node = lax.broadcasted_iota(jnp.int32, (size, PARTS * CAP), 0) + start
    return (node == rows).astype(F32).astype(BF)


def place():
    dom = lax.axis_index("dom")
    return dom // (NX * NC), lax.rem(dom // NC, NX), lax.rem(dom, NC), lax.axis_index("feat")


def device(z, x, c, f):
    return ((lax.rem(z, NZ) * NX + lax.rem(x, NX)) * NC + c, lax.rem(f, NF))


def remote(src, dst, send, recv, target):
    return pltpu.make_async_remote_copy(
        src_ref=src,
        dst_ref=dst,
        send_sem=send,
        recv_sem=recv,
        device_id=target,
        device_id_type=pl.DeviceIdType.MESH,
    )


def meet(targets):
    barrier = pltpu.get_barrier_semaphore()
    for target in targets:
        pl.semaphore_signal(
            barrier, inc=1, device_id=target, device_id_type=pl.DeviceIdType.MESH
        )
    return barrier


def slot_place():
    row = lax.broadcasted_iota(jnp.int32, (NX * CAP, NC * BLK), 0)
    lane = lax.broadcasted_iota(jnp.int32, (NX * CAP, NC * BLK), 1)
    want = (row // CAP) * (NC * CAP) + (lane // BLK) * CAP + row % CAP
    return (lane % BLK == want).astype(F32).astype(BF)


HALF = ROWS_DEV // 2
SLOTS = PARTS * CAP
TILES = NB * TPB
PAIRS = (TILES + EXT) // 2
POS = 640
SRC = 256
HUB0 = NB + NZ
WIDE = 2 * BLK
LOADS = 8
FACTOR = float(PARTS * ROWS_DEV) ** (-0.5)


def sort_tiles(col, row, idx):
    lane = lax.broadcasted_iota(jnp.int32, (TILES, SRC), 1)
    member = (col == lane).astype(F32)
    count = jnp.sum(member, axis=0, keepdims=True)
    pairs = jnp.floor((count + 1.0) * 0.5)
    before = lax.broadcasted_iota(jnp.int32, (SRC, SRC), 0) < lax.broadcasted_iota(
        jnp.int32, (SRC, SRC), 1
    )
    wide = jnp.broadcast_to(pairs, (16, SRC)).astype(BF)
    offset = jnp.dot(wide, before.astype(F32).astype(BF), preferred_element_type=F32)[0:1]
    mine = lax.broadcasted_iota(jnp.int32, (TILES, TILES), 0)
    other = lax.broadcasted_iota(jnp.int32, (TILES, TILES), 1)
    same = jnp.logical_and(col == row, other < mine).astype(F32)
    rank = jnp.sum(same, axis=1, keepdims=True)
    pos = 2.0 * jnp.sum(member * offset, axis=1, keepdims=True) + rank
    slot = lax.broadcasted_iota(jnp.int32, (TILES, POS), 1).astype(F32)
    tile = lax.broadcasted_iota(jnp.int32, (TILES, 1), 0)
    source = col.astype(F32)
    hit = (pos == slot).astype(F32)
    later = (pos + 2.0 == slot).astype(F32)

    def total(values):
        return jnp.sum(values, axis=0, keepdims=True)

    valid = total(hit)
    block = total(hit * (tile // TPB).astype(F32)) + float(NB) * (1.0 - valid)
    keep = (total(hit * source) == total(later * source)).astype(F32)
    idx[...] = jnp.zeros_like(idx)
    idx[0:1, :] = total(hit * tile.astype(F32)).astype(jnp.int32)
    idx[1:2, :] = block.astype(jnp.int32)
    idx[2:3, :] = keep.astype(jnp.int32)
    idx[3:4, 0:SRC] = jnp.maximum(offset + pairs - 1.0, 0.0).astype(jnp.int32)
    idx[4:5, 0:SRC] = (count > 0.0).astype(jnp.int32)
    idx[5:6, 0:TILES] = row


def entry(idx, row, at, most):
    return jnp.minimum(jnp.maximum(idx[row, at], 0), most)


def sage_kernel(
    hub_ref,
    tiles_hbm,
    hidden_ref,
    rows_ref,
    row_ref,
    col_ref,
    counts_ref,
    gl_in,
    ws_ref,
    wn_ref,
    logits_ref,
    gself_ref,
    gneigh_ref,
    out_ref,
    tiles,
    idx_v,
    idx,
    table,
    lives,
    live,
    gl_ref,
    wsend,
    w_ref,
    wt,
    total,
    outgoing,
    sibling,
    merged,
    planes,
    halo_ref,
    degree,
    scaled,
    runs,
    back_ref,
    hubg_ref,
    part_ref,
    mine_ref,
    logit,
    grads,
    pg_ref,
    y_mid,
    y_stage,
    y_last,
    pairs,
    arrive,
    stage,
    x_stage,
    x_got,
    xsum,
    k_first,
    k_mine,
    k_pair,
    g_pair,
    g_sum,
    g_x,
    g_row,
    g_z,
    g_last,
    g_final,
    t_sem,
    i_sem,
    gy_send,
    gy_recv,
    w_send,
    w_recv,
    hx_send,
    hx_recv,
    hz_send,
    hz_recv,
    hc_send,
    hc_recv,
    c_send,
    c_recv,
    z_send,
    z_recv,
    x_send,
    x_recv,
    y_send,
    y_recv,
    pc_send,
    pc_recv,
    r_send,
    r_recv,
    rx_send,
    rx_recv,
    kx_send,
    kx_recv,
    kz_send,
    kz_recv,
    kc_send,
    kc_recv,
    gc_send,
    gc_recv,
    gx_send,
    gx_recv,
    gz_send,
    gz_recv,
    gm_send,
    gm_recv,
):
    z, x, c, f = place()
    dom = lax.axis_index("dom")
    pair = device(z, x, 1 - c, f)
    group = z // 2
    swap = device(2 * f + lax.rem(z, 2), x, c, group)
    barrier = meet(
        [device(z, x, c, f + o) for o in range(1, NF)]
        + [device(z + o, x, c, f) for o in range(1, NZ)]
        + [device(z, x + o, c, f) for o in range(1, NX)]
        + [pair]
    )

    @pl.when(f != group)
    def _():
        meet([swap])

    loads = [
        pltpu.make_async_copy(
            tiles_hbm.at[pl.ds(i * (NB // LOADS), NB // LOADS)],
            tiles.at[pl.ds(i * (NB // LOADS), NB // LOADS)],
            t_sem.at[i],
        )
        for i in range(LOADS)
    ]
    for copy in loads:
        copy.start()
    sent = []

    def go(copy):
        copy.start()
        sent.append(copy)
        return copy

    gl_ref[f, 32:GP, :] = jnp.zeros((GP - 32, ROWS_DEV), BF)
    gl_ref[f, 0:GR, :] = gl_in[...]
    for g in range(NF):
        wsend[g] = jnp.zeros((GP, 2 * FD), BF)
        cols = slice(g * FD, (g + 1) * FD)
        wsend[g, 0:GR] = jnp.concatenate([ws_ref[:, cols], wn_ref[:, cols]], axis=1)
    w_ref[f] = wsend[f]

    def hub_at(core, plane, column, length):
        return pl.ds(HUB0 + core * 64 + plane * 8 + column * 2, length)

    for i in range(HB):
        wanted = hub_ref[0, i]
        piece = hidden_ref[:, 0:BLK]
        for b in range(1, NB):
            piece = jnp.where(wanted == b, hidden_ref[:, b * BLK : (b + 1) * BLK], piece)
        table[HUB0 + c * 64 + z * 8 + x * 2 + i] = piece
    for b in range(NB):
        table[b] = hidden_ref[:, b * BLK : (b + 1) * BLK]
    sort_tiles(col_ref[...], row_ref[...], idx_v)
    idx_copy = pltpu.make_async_copy(idx_v, idx, i_sem)
    idx_copy.start()

    pick = (lax.broadcasted_iota(jnp.int32, (16, PARTS), 1) == dom).astype(F32).astype(BF)
    got = lax.dot_general(
        pick, counts_ref[...].astype(F32).astype(BF), NT, preferred_element_type=F32
    )
    sender = lax.broadcasted_iota(jnp.int32, (PARTS, SLOTS), 0)
    column = lax.broadcasted_iota(jnp.int32, (PARTS, SLOTS), 1)
    spread_out = (column // CAP == sender).astype(F32).astype(BF)
    limit = jnp.dot(got.astype(BF), spread_out, preferred_element_type=F32)
    slot = lax.broadcasted_iota(jnp.int32, (16, SLOTS), 1) % CAP
    live[...] = (slot.astype(F32) < limit).astype(F32)
    lives[...] = jnp.ones_like(lives)
    for k in range(NZ):
        lives[NB + k] = live[:, k * BLK : (k + 1) * BLK].astype(BF)

    rows = rows_ref[...]
    total[...] = jnp.zeros_like(total)

    @pl.loop(0, ROWS_DEV // CHUNK)
    def _(i):
        start = pl.multiple_of(i * CHUNK, CHUNK)
        hot = one_hot_rows(rows, start, CHUNK)
        total[...] += jnp.dot(hidden_ref[:, pl.ds(start, CHUNK)], hot, preferred_element_type=F32)

    for k in range(NZ):
        piece = total[:, k * BLK : (k + 1) * BLK]
        zero = jnp.zeros_like(piece)
        both = jnp.concatenate(
            [jnp.where(c == 0, piece, zero), jnp.where(c == 1, piece, zero)], axis=0
        )
        outgoing[k] = both.T.astype(BF).reshape(NX, NC, CAP, BLK)
    idx_copy.wait()

    pl.semaphore_wait(barrier, jnp.where(f != group, NF + NZ + NX - 1, NF + NZ + NX - 2))

    def gy_copy(way, k, origin, half):
        part = gl_ref.at[lax.rem(origin + NF, NF), :, pl.ds(half * HALF, HALF)]
        target = device(z, x, c, f + (1 if way == 0 else NF - 1))
        return remote(part, part, gy_send.at[way, k], gy_recv.at[way, k], target)

    def gy_wait(way, k, distance, half):
        origin = lax.rem(f + (NF - distance if way == 0 else distance), NF)
        part = gl_ref.at[origin, :, pl.ds(half * HALF, HALF)]
        remote(part, part, gy_send.at[way, k], gy_recv.at[way, k], pair).wait_recv()

    for k in (0, 1):
        go(gy_copy(0, k, f, k))
        go(gy_copy(1, k, f, 1 - k))
    for o in range(1, NX):
        part = table.at[hub_at(c, z, x, HB)]
        go(remote(part, part, hx_send.at[o - 1], hx_recv.at[o - 1], device(z, x + o, c, f)))
    to_pair = go(remote(outgoing.at[:, :, 1 - c], sibling, c_send, c_recv, pair))
    for o in range(1, NF):
        go(
            remote(
                wsend.at[lax.rem(f + o, NF)],
                w_ref.at[f],
                w_send.at[o - 1],
                w_recv.at[o - 1],
                device(z, x, c, f + o),
            )
        )

    def hz_copy(way, k, half):
        origin = lax.rem(z + (NZ - k if way == 0 else k), NZ)
        part = table.at[hub_at(c, origin, 2 * half, 2 * HB)]
        target = device(z + (1 if way == 0 else NZ - 1), x, c, f)
        return remote(part, part, hz_send.at[way, k, half], hz_recv.at[way, k, half], target)

    def hz_wait(way, k, half):
        origin = lax.rem(z + (NZ - k - 1 if way == 0 else k + 1), NZ)
        part = table.at[hub_at(c, origin, 2 * half, 2 * HB)]
        remote(part, part, hz_send.at[way, k, half], hz_recv.at[way, k, half], pair).wait_recv()

    def hc_copy(k, half):
        part = table.at[hub_at(c, lax.rem(z + k, NZ), 2 * half, 2 * HB)]
        return remote(part, part, hc_send.at[k, half], hc_recv.at[k, half], pair)

    def hc_wait(k, half):
        part = table.at[hub_at(1 - c, lax.rem(z + k, NZ), 2 * half, 2 * HB)]
        remote(part, part, hc_send.at[k, half], hc_recv.at[k, half], pair).wait_recv()

    def ring(k):
        for half in (0, 1):
            for way in (0, 1):
                part = half if way == 0 else 1 - half
                if k == 3 and part != way:
                    continue
                hz_wait(way, k, part)
                if k < 2 or (k == 2 and part == way):
                    go(hz_copy(way, k + 1, part))
                go(hc_copy(NZ - k - 1 if way == 0 else k + 1, part))

    def block_weights(b):
        return jnp.concatenate([tiles[b, j] for j in range(TPB)], axis=1)

    def degrees(part):
        for i in range(part * LOADS // 4, (part + 1) * LOADS // 4):
            loads[i].wait()

        @pl.loop(part * (NB // 4), (part + 1) * (NB // 4))
        def _(b):
            alive = jnp.concatenate([lives[entry(idx, 5, b * TPB + j, EXT - 1)] for j in range(TPB)], axis=1)
            degree[b] = lax.dot_general(
                alive, block_weights(b), NT, preferred_element_type=F32
            )[0:8]

    degrees(0)
    for o in range(1, NX):
        part = table.at[hub_at(c, z, lax.rem(x + NX - o, NX), HB)]
        remote(part, part, hx_send.at[o - 1], hx_recv.at[o - 1], pair).wait_recv()
    for half in (0, 1):
        go(hz_copy(0, 0, half))
        go(hz_copy(1, 0, 1 - half))
    for half in (0, 1):
        go(hc_copy(0, half))
    to_pair.wait_recv()
    merged[...] = outgoing[:, :, c] + sibling[...]
    for o in range(1, NZ):
        go(
            remote(
                merged.at[lax.rem(z + o, NZ)],
                planes.at[z],
                z_send.at[o - 1],
                z_recv.at[o - 1],
                device(z + o, x, c, f),
            )
        )
    planes[z] = merged[z]
    degrees(1)
    gy_wait(0, 0, 1, 0)
    go(gy_copy(0, 2, f - 1, 0))
    gy_wait(1, 0, 1, 1)
    go(gy_copy(1, 2, f + 1, 1))
    ring(0)
    degrees(2)
    for o in range(1, NZ):
        part = planes.at[lax.rem(z + NZ - o, NZ)]
        remote(part, part, z_send.at[o - 1], z_recv.at[o - 1], pair).wait_recv()
    for o in range(1, NX):
        go(
            remote(
                planes.at[:, lax.rem(x + o, NX)],
                halo_ref.at[x],
                x_send.at[o - 1],
                x_recv.at[o - 1],
                device(z, x + o, c, f),
            )
        )
    halo_ref[x] = planes[:, x]
    ring(1)
    degrees(3)
    for o in range(1, NX):
        part = halo_ref.at[lax.rem(x + NX - o, NX)]
        remote(part, part, x_send.at[o - 1], x_recv.at[o - 1], pair).wait_recv()
    place_slots = slot_place()
    for k in range(NZ):
        res = lax.dot_general(
            halo_ref[:, k].reshape(NX * CAP, BLK), place_slots, TN, preferred_element_type=F32
        )
        alive = live[0:1, k * BLK : (k + 1) * BLK]
        table[NB + k] = ((res[0:FD, 0:BLK] + res[FD:, BLK:]) * alive).astype(BF)
    for o in range(1, NF):
        part = w_ref.at[lax.rem(f + NF - o, NF)]
        remote(part, part, w_send.at[o - 1], w_recv.at[o - 1], pair).wait_recv()
    wt[...] = w_ref[...].reshape(NF * GP, 2 * FD).astype(F32).T.astype(BF)
    grads[...] = jnp.zeros_like(grads)
    scaled[NB] = jnp.zeros((FD, BLK), BF)
    ring(2)
    gy_wait(0, 1, 1, 1)
    gy_wait(1, 1, 1, 0)
    gy_wait(0, 2, 2, 0)
    gy_wait(1, 2, 2, 1)

    def columns(step):
        return pl.ds(pl.multiple_of(step * WIDE, WIDE), WIDE)

    @pl.loop(0, NB // 2)
    def _(step):
        gl = gl_ref[:, :, columns(step)].reshape(NF * GP, WIDE)
        both = jnp.dot(wt[...], gl, preferred_element_type=F32)
        out_ref[:, columns(step)] = both[0:FD]
        for k in range(2):
            b = step * 2 + k
            part = both[FD:, k * BLK : (k + 1) * BLK] / degree[b, 0:1]
            scaled[b] = part.astype(BF)

    def push(k, run):
        flat = tiles.reshape(TILES, BLK, BLK)
        spots = (2 * k, 2 * k + 1)
        left = jnp.concatenate([scaled[entry(idx, 1, q, NB)] for q in spots], axis=1)
        right = jnp.concatenate([flat[entry(idx, 0, q, TILES - 1)] for q in spots], axis=0)
        run = jnp.where(idx[2, 2 * k] == 1, run, 0.0)
        run = run + jnp.dot(left, right, preferred_element_type=F32)
        runs[k] = run
        return run

    lax.fori_loop(0, PAIRS, push, jnp.zeros((FD, BLK), F32), unroll=6)

    def returned(source):
        return jnp.where(idx[4, source] == 1, runs[entry(idx, 3, source, PAIRS - 1)], 0.0)

    @pl.loop(0, PARTS * HB)
    def _(h):
        hubg_ref[h] = returned(HUB0 + h).astype(BF)

    def hub_rows(core, plane):
        return pl.ds(core * 64 + plane * 8, 8)

    order = (4, 3, 5, 2, 6, 1, 7, 0)
    hub_pair = {}
    for o in order:
        dest = lax.rem(z + o, NZ)
        hub_pair[o] = go(
            remote(
                hubg_ref.at[hub_rows(1 - c, dest)],
                pairs.at[dest],
                pc_send.at[o],
                pc_recv.at[o],
                pair,
            )
        )
    for k in range(NZ):
        block = (returned(NB + k) * live[0:1, k * BLK : (k + 1) * BLK]).astype(BF)
        zero = jnp.zeros_like(block)
        wide = jnp.concatenate(
            [jnp.concatenate([block, zero], axis=1), jnp.concatenate([zero, block], axis=1)],
            axis=0,
        )
        back = lax.dot_general(place_slots, wide, NT, preferred_element_type=F32)
        back_ref[:, k] = back.astype(BF).reshape(NX, CAP, BLK)
    kx = [
        go(
            remote(
                back_ref.at[lax.rem(x + o, NX)],
                k_first.at[x],
                kx_send.at[o - 1],
                kx_recv.at[o - 1],
                device(z, x + o, c, f),
            )
        )
        for o in range(1, NX)
    ]
    k_first[x] = back_ref[x]

    hops = {}

    def hub_step(k):
        distance = NZ // 2 - k
        for o in (distance, NZ - distance):
            if k > 0 or o == distance:
                if (o, "got") not in hops:
                    hub_pair[o].wait_recv()
                    hops[o, "got"] = True
        for half in (0, 1):
            for way in (0, 1):
                h = half if way == 0 else 1 - half
                if k == 0 and h != way:
                    continue
                dest = lax.rem(z + (distance if way == 0 else NZ - distance), NZ)
                value = hubg_ref[pl.ds(c * 64 + dest * 8 + 4 * h, 4)].astype(F32)
                value = value + pairs[dest, 4 * h : 4 * h + 4].astype(F32)
                if k > 1 or (k == 1 and h == way):
                    hops[way, k - 1, h].wait_recv()
                    value = value + arrive[way, k - 1, h].astype(F32)
                stage[way, k, h] = value.astype(BF)
                hops[way, k, h] = go(
                    remote(
                        stage.at[way, k, h],
                        arrive.at[way, k, h],
                        r_send.at[way, k, h],
                        r_recv.at[way, k, h],
                        device(z + (1 if way == 0 else NZ - 1), x, c, f),
                    )
                )

    hub_step(0)
    ring(3)
    for k in range(NZ):
        for half in (0, 1):
            hc_wait(k, half)

    def forward(part):
        @pl.loop(part * (NB // 8), (part + 1) * (NB // 8))
        def _(step):
            gl = gl_ref[:, :, columns(step)].reshape(NF * GP, WIDE)
            means = []
            for k in range(2):
                b = step * 2 + k
                picked = jnp.concatenate(
                    [table[entry(idx, 5, b * TPB + j, EXT - 1)] for j in range(TPB)], axis=1
                )
                summed = lax.dot_general(
                    picked, block_weights(b), NT, preferred_element_type=F32
                )
                means.append((summed / degree[b, 0:1]).astype(BF))
            both = jnp.concatenate(
                [hidden_ref[:, columns(step)], jnp.concatenate(means, axis=1)], axis=0
            )
            logit[...] = jnp.dot(
                w_ref[...].reshape(NF * GP, 2 * FD), both, preferred_element_type=F32
            ).reshape(NF, GP, WIDE)
            part_ref[:, :, columns(step)] = logit[...].astype(BF)
            mine_ref[:, columns(step)] = logit[f]
            grads[...] += lax.dot_general(both, gl, NT, preferred_element_type=F32)

    def y_cols(half):
        return pl.ds(half * HALF, HALF)

    def y_copy(way, k, src, dst):
        target = device(z, x, c, f + (1 if way == 0 else NF - 1))
        return remote(src, dst, y_send.at[way, k], y_recv.at[way, k], target)

    def y_part(distance, half):
        return part_ref.at[lax.rem(f + distance, NF), :, y_cols(half)]

    y0, y1, y2 = {}, {}, {}

    def y_start(half):
        y0[half] = go(y_copy(half, 0, y_part(2, half), y_mid.at[half]))
        way = 1 - half
        y1[way] = go(
            y_copy(way, 1, y_part(1 if way == 0 else NF - 1, half), y_last.at[way, half])
        )

    def y_pass(w):
        y0[w].wait_recv()
        near = lax.rem(f + (1 if w == 0 else NF - 1), NF)
        value = part_ref[near, :, y_cols(w)].astype(F32) + y_mid[w].astype(F32)
        y_stage[w] = value.astype(BF)
        y2[w] = go(y_copy(w, 2, y_stage.at[w], y_last.at[w, w]))

    forward(0)
    for copy in kx:
        copy.wait_recv()
    kz = [
        go(
            remote(
                k_first.at[:, lax.rem(z + o, NZ)],
                k_mine.at[z],
                kz_send.at[o - 1],
                kz_recv.at[o - 1],
                device(z + o, x, c, f),
            )
        )
        for o in range(1, NZ)
    ]
    k_mine[z] = k_first[:, z]
    forward(1)
    y_start(0)
    hub_step(1)
    forward(2)
    forward(3)
    y_start(1)

    scores = grads[...] * FACTOR
    for j in range(16):
        rows_j = slice(4 * j, 4 * j + 4)
        far_j = slice(FD + 4 * j, FD + 4 * j + 4)
        both_j = jnp.concatenate([scores[rows_j], scores[far_j]], axis=0)
        for g in range(NF):
            pg_ref[2 * g + j // 8, j // 2 % 4, j % 2] = jnp.concatenate(
                [both_j[:, g * GP : (g + 1) * GP], jnp.zeros((8, BLK - GP), F32)], axis=1
            )
    g_to_pair = go(remote(pg_ref.at[:, :, 1 - c], g_pair, gc_send, gc_recv, pair))
    for copy in kz:
        copy.wait_recv()
    kc = go(remote(k_mine, k_pair, kc_send, kc_recv, pair))
    hub_step(2)
    y_pass(0)

    g_to_pair.wait_recv()
    g_sum[...] = pg_ref[:, :, c] + g_pair[...]
    gx = [
        go(
            remote(
                g_sum.at[:, lax.rem(x + o, NX)],
                g_x.at[o - 1],
                gx_send.at[o - 1],
                gx_recv.at[o - 1],
                device(z, x + o, c, f),
            )
        )
        for o in range(1, NX)
    ]

    kc.wait_recv()
    flat_back = []
    for k in range(NZ):
        a, b = k_mine[k], k_pair[k]
        first = jnp.where(c == 0, a, b)
        second = jnp.where(c == 0, b, a)
        turned = jnp.stack([first, second], axis=1).reshape(BLK, BLK).astype(F32).T
        flat_back.append(jnp.where(c == 0, turned[0:FD], turned[FD:]).astype(BF))
    back = jnp.concatenate(flat_back, axis=1)

    def scatter(first, last):
        @pl.loop(first, last)
        def _(i):
            start = pl.multiple_of(i * CHUNK, CHUNK)
            hot = one_hot_rows(rows, start, CHUNK)
            got = lax.dot_general(back, hot, NT, preferred_element_type=F32)
            own = [returned(i * (CHUNK // BLK) + k) for k in range(CHUNK // BLK)]
            out_ref[:, pl.ds(start, CHUNK)] += got + jnp.concatenate(own, axis=1)

    scatter(0, 2)
    hub_step(3)
    y_pass(1)
    for copy in gx:
        copy.wait_recv()
    g_row[...] = g_sum[:, x] + g_x[0] + g_x[1] + g_x[2]
    gz = [
        go(
            remote(
                g_row.at[lax.rem(z + o, NZ)],
                g_z.at[o - 1],
                gz_send.at[o - 1],
                gz_recv.at[o - 1],
                device(z + o, x, c, f),
            )
        )
        for o in range(1, NZ)
    ]
    scatter(2, ROWS_DEV // CHUNK)

    for copy in gz:
        copy.wait_recv()
    done = g_row[z]
    for o in range(1, NZ):
        done = done + g_z[o - 1]
    g_last[...] = done
    move = remote(g_last, g_final, gm_send, gm_recv, swap)

    @pl.when(f != group)
    def _():
        move.start()

    @pl.when(f == group)
    def _():
        g_final[...] = done

    hub_pair[0].wait_recv()
    for half in (0, 1):
        span = slice(4 * half, 4 * half + 4)
        value = hubg_ref[pl.ds(c * 64 + z * 8 + 4 * half, 4)].astype(F32)
        value = value + pairs[z, span].astype(F32)
        for way in (0, 1):
            hops[way, 3, half].wait_recv()
            value = value + arrive[way, 3, half].astype(F32)
        xsum[span] = value
    x_stage[...] = xsum[...].astype(BF)
    rx = [
        go(
            remote(
                x_stage.at[pl.ds(lax.rem(x + o, NX) * HB, HB)],
                x_got.at[o - 1],
                rx_send.at[o - 1],
                rx_recv.at[o - 1],
                device(z, x + o, c, f),
            )
        )
        for o in range(1, NX)
    ]

    for w in (0, 1):
        y1[w].wait_recv()
        y2[w].wait_recv()
    for half in (0, 1):
        cols = y_cols(half)
        value = mine_ref[0:GR, cols]
        for w in (0, 1):
            value = value + y_last[w, half, 0:GR].astype(F32)
        logits_ref[:, cols] = value.astype(BF)

    for copy in rx:
        copy.wait_recv()
    summed = xsum[pl.ds(x * HB, HB)]
    for o in range(1, NX):
        summed = summed + x_got[o - 1].astype(F32)
    for b in range(NB):
        cols = slice(b * BLK, (b + 1) * BLK)
        value = out_ref[:, cols]
        for i in range(HB):
            value = jnp.where(hub_ref[0, i] == b, value + summed[i], value)
        out_ref[:, cols] = value

    @pl.when(f != group)
    def _():
        move.wait()

    turned = jnp.concatenate([g_final[...], jnp.zeros((BLK - 8, BLK), F32)], axis=0).T
    gself_ref[...] = turned[0:GR, 0:4]
    gneigh_ref[...] = turned[0:GR, 4:8]
    for copy in sent:
        copy.wait_send()


def sage(hub_blocks, tiles, hidden, rows, src_row, src_col, counts, gl, w_self, w_neigh):
    dma = pltpu.SemaphoreType.DMA
    outs = (
        jax.ShapeDtypeStruct((GR, ROWS_DEV), BF),
        jax.ShapeDtypeStruct((GR, 4), F32),
        jax.ShapeDtypeStruct((GR, 4), F32),
        jax.ShapeDtypeStruct((FD, ROWS_DEV), F32),
    )

    def both(*shape):
        return [dma(shape), dma(shape)]

    return pl.pallas_call(
        sage_kernel,
        out_shape=outs,
        in_specs=[spec(pltpu.SMEM), spec(pl.ANY)] + [spec()] * 8,
        out_specs=(spec(),) * 4,
        scratch_shapes=[
            VM((NB, TPB, BLK, BLK), BF),
            VM((8, POS), jnp.int32),
            pltpu.SMEM((8, POS), jnp.int32),
            VM((EXT, FD, BLK), BF),
            VM((EXT, 16, BLK), BF),
            VM((16, SLOTS), F32),
            VM((NF, GP, ROWS_DEV), BF),
            VM((NF, GP, 2 * FD), BF),
            VM((NF, GP, 2 * FD), BF),
            VM((2 * FD, NF * GP), BF),
            VM((FD, SLOTS), F32),
            VM((NZ, NX, NC, CAP, BLK), BF),
            VM((NZ, NX, CAP, BLK), BF),
            VM((NZ, NX, CAP, BLK), BF),
            VM((NZ, NX, CAP, BLK), BF),
            VM((NX, NZ, CAP, BLK), BF),
            VM((NB, 8, BLK), F32),
            VM((NB + 1, FD, BLK), BF),
            VM((PAIRS, FD, BLK), F32),
            VM((NX, NZ, CAP, BLK), BF),
            VM((PARTS * HB, FD, BLK), BF),
            VM((NF, GP, ROWS_DEV), BF),
            VM((GP, ROWS_DEV), F32),
            VM((NF, GP, WIDE), F32),
            VM((2 * FD, NF * GP), F32),
            VM((NZ, NX, NC, 8, BLK), F32),
            VM((2, GP, HALF), BF),
            VM((2, GP, HALF), BF),
            VM((2, 2, GP, HALF), BF),
            VM((NZ, 8, FD, BLK), BF),
            VM((2, 4, 2, 4, FD, BLK), BF),
            VM((2, 4, 2, 4, FD, BLK), BF),
            VM((8, FD, BLK), BF),
            VM((NX - 1, HB, FD, BLK), BF),
            VM((8, FD, BLK), F32),
            VM((NX, NZ, CAP, BLK), BF),
            VM((NZ, NX, CAP, BLK), BF),
            VM((NZ, NX, CAP, BLK), BF),
            VM((NZ, NX, 8, BLK), F32),
            VM((NZ, NX, 8, BLK), F32),
            VM((NX - 1, NZ, 8, BLK), F32),
            VM((NZ, 8, BLK), F32),
            VM((NZ - 1, 8, BLK), F32),
            VM((8, BLK), F32),
            VM((8, BLK), F32),
            dma((LOADS,)),
            dma,
        ]
        + both(2, 3)
        + both(3)
        + both(3)
        + both(2, 4, 2)
        + both(8, 2)
        + [dma, dma]
        + both(7)
        + both(3)
        + both(2, 3)
        + both(8)
        + both(2, 4, 2)
        + both(3)
        + both(3)
        + both(7)
        + [dma, dma]
        + [dma, dma]
        + both(3)
        + both(7)
        + [dma, dma],
        compiler_params=pltpu.CompilerParams(
            collective_id=0, has_side_effects=True, vmem_limit_bytes=60 << 20
        ),
    )(hub_blocks, tiles, hidden, rows, src_row, src_col, counts, gl, w_self, w_neigh)


def local(
    hidden,
    tiles,
    tile_src,
    hub_blocks,
    halo_rows,
    halo_counts,
    weight_self,
    weight_neigh,
    grad_logits,
):
    rows = halo_rows.reshape(1, PARTS * CAP)
    hub = tile_src - HUB0
    moved = HUB0 + hub // 2 % 2 * 64 + hub // 16 * 8 + hub // 4 % 4 * 2 + hub % 2
    src = jnp.where(tile_src < HUB0, tile_src, moved)
    return sage(
        hub_blocks,
        tiles,
        hidden,
        rows,
        src.reshape(1, TILES),
        src.reshape(TILES, 1),
        halo_counts,
        grad_logits,
        weight_self,
        weight_neigh,
    )


def solution(mesh):
    placed = (
        P("feat", "dom"),
        P("dom", None, None, None),
        P("dom", None),
        P("dom", None),
        P("dom", None, None),
        P(),
        P("feat", None),
        P("feat", None),
        P("feat", "dom"),
    )
    return jax.shard_map(
        local,
        mesh=mesh,
        in_specs=placed,
        out_specs=(P("feat", "dom"), P("feat", "dom"), P("feat", "dom"), P("feat", "dom")),
        check_vma=False,
    )
```

time: 602 us -> 87.6 us (0.15)
  waiting for transfers between devices: 391 us -> 0 us
  other arithmetic: 78.8 us -> 0.73 us
  Pallas kernels: 0 us -> 76 us
  matrix products: 45.2 us -> 0 us
  local copies, waits for them, and re-layouts: 43.6 us -> 9.82 us
  starting transfers between devices: 23.4 us -> 0 us
  between operations: 15.2 us -> 0.64 us
    reduce_scatter x3 -> x0, waiting for transfers between devices: 229 us -> none  [the longest x1 134 us: local(): lax.psum_scatter(hub_grad, 'dom', scatter_dimension=1, tiled=True)]
    all_gather x3 -> x0, waiting for transfers between devices: 81.3 us -> none  [the longest x1 48.5 us: local(): hub_table = lax.all_gather(hub_piece, 'dom', axis=1, tiled=True)]
    unnamed x8 -> x0, waiting for transfers between devices: 78.9 us -> none
    pallas_call x0 -> x1, Pallas kernels: none -> 76 us  [sage(): pl.pallas_call(sage_kernel, out_shape=outs, in_specs=[spec(pltpu.SMEM), s...]
    scatter-add x3 -> x0, other arithmetic: 68.2 us -> none  [the longest x1 59.9 us: local(): jnp.zeros((columns, sources_table.shape[1], BLK), jnp.float32)]
    dot_general x9 -> x0, matrix products: 45.2 us -> none  [the longest x1 11.3 us: local(): jnp.einsum('bjds,cbd->cbjs', tiles, scaled, preferred_element_type=jnp.fl...]
    all_to_all x2 -> x0, starting transfers between devices: 22.7 us -> none  [the longest x1 11.9 us: local(): lax.all_to_all(outgoing, 'dom', split_axis=1, concat_axis=1, tiled=True)]
    gather x5 -> x0, local copies, waits for them, and re-layouts: 18.3 us -> none  [the longest x1 13.3 us: local(): jnp.take(sources_table, sources, axis=1).reshape(columns, NB, TPB, BLK)]
  transfers between devices with their start and end apart: 9 -> 0, of which waited for: 7 -> 0; matrix products, arithmetic and copies ran while one was open for 27% -> 0% of each run, Pallas kernels for 0% -> 0%
where the time goes in v4:
time: 87.6 us; the launch traced here: 87.2 us
  Pallas kernels  76 us (87%)
  local copies, waits for them, and re-layouts  9.82 us (11%)
    pallas_call x1, Pallas kernels, sage(): pl.pallas_call(sage_kernel, out_shape=outs, in_specs=[spec(pltpu.SMEM), s...  76 us
    unnamed x3, local copies, waits for them, and re-layouts  4.81 us
    pallas_call x2, local copies, waits for them, and re-layouts, sage(): pl.pallas_call(sage_kernel, out_shape=outs, in_specs=[spec(pltpu.SMEM), s...  2.78 us

profile of v4, /device:TPU:16, one launch (start us, length us, event | category | flops | bytes accessed | tf_op | source)
XLA Modules:
  0.0 87.2 jit_solution(18203169338462643951)
XLA Ops:
  0.6 0.7 compare_select_fusion
  1.4 0.1 copy.19
  1.4 0.7 reshape.18.row_ref
  2.1 0.8 copy.18
  2.9 0.7 reshape.17.rows_ref
  3.6 0.8 reshape.20.col_ref
  4.4 76.0 %shard_map.120 = (bf16[43,4096]{1,0:T(8,128)(2,1)}, f32[43,4]{1,0:T(8,128)}, f32[43,4]{1,0:T(8,128)}, f32[64,4096]{1,0:T(8,128)}) custom-call(s32[1,2]{1,0:T(1,128)} %hub_ref.1, bf16[32,12,128,128]{3,2,1,0:T(8,128)(2,1)} %tiles_hbm.1, bf16[64,4096]{1,0:T(8,128)(2,1)} %hidden_ref.1, s32[1,1024]{1,0:T(1,128)} %reshape.17.rows_ref, s32[1,384]{1,0:T(1,128)} %reshape.18.row_ref, ...), custom_call_target="tpu_custom_call" | custom-call | tf_op jit(solution)/shard_map/pallas_call | solution.py:791
  80.4 1.4 %copy.22 = f32[43,4]{0,1:T(4,128)} copy(f32[43,4]{1,0:T(8,128)} %get-tuple-element.9) | data formatting | bytes 1376 | tf_op jit(solution)/shard_map/pallas_call | solution.py:791
  81.8 1.4 %copy.23 = f32[43,4]{0,1:T(4,128)} copy(f32[43,4]{1,0:T(8,128)} %get-tuple-element.10) | data formatting | bytes 1376 | tf_op jit(solution)/shard_map/pallas_call | solution.py:791
  83.2 1.8 %copy.26 = bf16[43,4096]{1,0:T(8,128)(2,1)} copy(bf16[43,4096]{1,0:T(8,128)(2,1)} %get-tuple-element.16) | data formatting | bytes 704512
  84.9 2.3 %copy.27 = f32[64,4096]{1,0:T(8,128)} copy(f32[64,4096]{1,0:T(8,128)} %get-tuple-element.19) | data formatting | bytes 2097152

commit v5 on v4

--- a/solution.py
+++ b/solution.py
@@ -127,16 +127,15 @@
     hub_ref,
     tiles_hbm,
     hidden_ref,
-    rows_ref,
-    row_ref,
-    col_ref,
+    halo_rows_ref,
+    src_ref,
     counts_ref,
     gl_in,
     ws_ref,
     wn_ref,
     logits_ref,
-    gself_ref,
-    gneigh_ref,
+    score_ref,
+    sum_ref,
     out_ref,
     tiles,
     idx_v,
@@ -173,6 +172,11 @@
     x_stage,
     x_got,
     xsum,
+    b_stage,
+    b_got,
+    bsum,
+    bz_stage,
+    bz_got,
     k_first,
     k_mine,
     k_pair,
@@ -209,6 +213,10 @@
     r_recv,
     rx_send,
     rx_recv,
+    bx_send,
+    bx_recv,
+    bz_send,
+    bz_recv,
     kx_send,
     kx_recv,
     kz_send,
@@ -276,7 +284,25 @@
         table[HUB0 + c * 64 + z * 8 + x * 2 + i] = piece
     for b in range(NB):
         table[b] = hidden_ref[:, b * BLK : (b + 1) * BLK]
-    sort_tiles(col_ref[...], row_ref[...], idx_v)
+    source = src_ref[...]
+    hub = jnp.maximum(source - HUB0, 0)
+    moved = HUB0 + (hub // 2 % 2) * 64 + (hub // 16) * 8 + (hub // 4 % 4) * 2 + hub % 2
+    source = jnp.where(source < HUB0, source, moved).astype(F32).astype(BF)
+    tile_lane = lax.broadcasted_iota(jnp.int32, (NB, TILES), 1)
+    of_block = lax.broadcasted_iota(jnp.int32, (NB, TILES), 0) == tile_lane // TPB
+    row = jnp.dot(source, of_block.astype(F32).astype(BF), preferred_element_type=F32)
+    at = lax.broadcasted_iota(jnp.int32, (TPB, TILES), 1) % TPB
+    row = jnp.where(at == lax.broadcasted_iota(jnp.int32, (TPB, TILES), 0), row, 0.0)
+    row = jnp.sum(row, axis=0, keepdims=True).astype(jnp.int32)
+    tile_row = lax.broadcasted_iota(jnp.int32, (TILES, NB), 0)
+    of_block = lax.broadcasted_iota(jnp.int32, (TILES, NB), 1) == tile_row // TPB
+    col = lax.dot_general(
+        of_block.astype(F32).astype(BF), source, NT, preferred_element_type=F32
+    )
+    at = lax.broadcasted_iota(jnp.int32, (TILES, TPB), 0) % TPB
+    col = jnp.where(at == lax.broadcasted_iota(jnp.int32, (TILES, TPB), 1), col, 0.0)
+    col = jnp.sum(col, axis=1, keepdims=True).astype(jnp.int32)
+    sort_tiles(col, row, idx_v)
     idx_copy = pltpu.make_async_copy(idx_v, idx, i_sem)
     idx_copy.start()
 
@@ -294,7 +320,15 @@
     for k in range(NZ):
         lives[NB + k] = live[:, k * BLK : (k + 1) * BLK].astype(BF)
 
-    rows = rows_ref[...]
+    high = halo_rows_ref[...] // FD
+    low = halo_rows_ref[...] - high * FD
+    rows = sum(
+        scale
+        * jnp.dot(part.astype(F32).astype(BF), spread_out, preferred_element_type=F32)
+        for part, scale in ((high, float(FD)), (low, 1.0))
+    )
+    at = lax.broadcasted_iota(jnp.int32, (CAP, SLOTS), 0)
+    rows = jnp.sum(jnp.where(slot == at, rows, 0.0), axis=0, keepdims=True).astype(jnp.int32)
     total[...] = jnp.zeros_like(total)
 
     @pl.loop(0, ROWS_DEV // CHUNK)
@@ -447,7 +481,6 @@
     wt[...] = w_ref[...].reshape(NF * GP, 2 * FD).astype(F32).T.astype(BF)
     grads[...] = jnp.zeros_like(grads)
     scaled[NB] = jnp.zeros((FD, BLK), BF)
-    ring(2)
     gy_wait(0, 1, 1, 1)
     gy_wait(1, 1, 1, 0)
     gy_wait(0, 2, 2, 0)
@@ -466,6 +499,8 @@
             part = both[FD:, k * BLK : (k + 1) * BLK] / degree[b, 0:1]
             scaled[b] = part.astype(BF)
 
+    ring(2)
+
     def push(k, run):
         flat = tiles.reshape(TILES, BLK, BLK)
         spots = (2 * k, 2 * k + 1)
@@ -476,7 +511,7 @@
         runs[k] = run
         return run
 
-    lax.fori_loop(0, PAIRS, push, jnp.zeros((FD, BLK), F32), unroll=6)
+    lax.fori_loop(0, PAIRS, push, jnp.zeros((FD, BLK), F32), unroll=23)
 
     def returned(source):
         return jnp.where(idx[4, source] == 1, runs[entry(idx, 3, source, PAIRS - 1)], 0.0)
@@ -525,22 +560,30 @@
     k_first[x] = back_ref[x]
 
     hops = {}
+    seen = set()
+
+    def from_pair(o):
+        if o not in seen:
+            seen.add(o)
+            hub_pair[o].wait_recv()
+
+    def hub_part(plane, first, length, half):
+        low, high = half * FD // 2, (half + 1) * FD // 2
+        mine = hubg_ref[pl.ds(c * 64 + plane * 8 + first, length), low:high]
+        other = pairs[plane, pl.ds(first, length), low:high]
+        return mine.astype(F32) + other.astype(F32)
 
     def hub_step(k):
         distance = NZ // 2 - k
-        for o in (distance, NZ - distance):
-            if k > 0 or o == distance:
-                if (o, "got") not in hops:
-                    hub_pair[o].wait_recv()
-                    hops[o, "got"] = True
+        from_pair(distance)
+        from_pair(NZ - distance)
         for half in (0, 1):
             for way in (0, 1):
                 h = half if way == 0 else 1 - half
                 if k == 0 and h != way:
                     continue
                 dest = lax.rem(z + (distance if way == 0 else NZ - distance), NZ)
-                value = hubg_ref[pl.ds(c * 64 + dest * 8 + 4 * h, 4)].astype(F32)
-                value = value + pairs[dest, 4 * h : 4 * h + 4].astype(F32)
+                value = hub_part(dest, 4 * h, 4, 0)
                 if k > 1 or (k == 1 and h == way):
                     hops[way, k - 1, h].wait_recv()
                     value = value + arrive[way, k - 1, h].astype(F32)
@@ -556,6 +599,27 @@
                 )
 
     hub_step(0)
+    for o in range(NZ):
+        from_pair(o)
+    bx = []
+    for o in range(1, NX):
+        column_o = lax.rem(x + o, NX)
+
+        @pl.loop(0, NZ)
+        def _(plane):
+            b_stage[o - 1, plane] = hub_part(plane, column_o * HB, HB, 1).astype(BF)
+
+        bx.append(
+            go(
+                remote(
+                    b_stage.at[o - 1],
+                    b_got.at[o - 1],
+                    bx_send.at[o - 1],
+                    bx_recv.at[o - 1],
+                    device(z, x + o, c, f),
+                )
+            )
+        )
     ring(3)
     for k in range(NZ):
         for half in (0, 1):
@@ -630,7 +694,31 @@
     forward(1)
     y_start(0)
     hub_step(1)
+    for copy in bx:
+        copy.wait_recv()
+
+    @pl.loop(0, NZ)
+    def _(plane):
+        value = hub_part(plane, x * HB, HB, 1)
+        for o in range(1, NX):
+            value = value + b_got[o - 1, plane].astype(F32)
+        bsum[plane] = value
+        bz_stage[plane] = value.astype(BF)
+
+    bz = [
+        go(
+            remote(
+                bz_stage.at[lax.rem(z + o, NZ)],
+                bz_got.at[o - 1],
+                bz_send.at[o - 1],
+                bz_recv.at[o - 1],
+                device(z + o, x, c, f),
+            )
+        )
+        for o in range(1, NZ)
+    ]
     forward(2)
+    hub_step(2)
     forward(3)
     y_start(1)
 
@@ -647,7 +735,7 @@
     for copy in kz:
         copy.wait_recv()
     kc = go(remote(k_mine, k_pair, kc_send, kc_recv, pair))
-    hub_step(2)
+    hub_step(3)
     y_pass(0)
 
     g_to_pair.wait_recv()
@@ -684,8 +772,25 @@
             own = [returned(i * (CHUNK // BLK) + k) for k in range(CHUNK // BLK)]
             out_ref[:, pl.ds(start, CHUNK)] += got + jnp.concatenate(own, axis=1)
 
-    scatter(0, 2)
-    hub_step(3)
+    for half in (0, 1):
+        value = hub_part(z, 4 * half, 4, 0)
+        for way in (0, 1):
+            hops[way, 3, half].wait_recv()
+            value = value + arrive[way, 3, half].astype(F32)
+        xsum[4 * half : 4 * half + 4] = value
+    x_stage[...] = xsum[...].astype(BF)
+    rx = [
+        go(
+            remote(
+                x_stage.at[pl.ds(lax.rem(x + o, NX) * HB, HB)],
+                x_got.at[o - 1],
+                rx_send.at[o - 1],
+                rx_recv.at[o - 1],
+                device(z, x + o, c, f),
+            )
+        )
+        for o in range(1, NX)
+    ]
     y_pass(1)
     for copy in gx:
         copy.wait_recv()
@@ -702,7 +807,7 @@
         )
         for o in range(1, NZ)
     ]
-    scatter(2, ROWS_DEV // CHUNK)
+    scatter(0, ROWS_DEV // CHUNK)
 
     for copy in gz:
         copy.wait_recv()
@@ -720,28 +825,18 @@
     def _():
         g_final[...] = done
 
-    hub_pair[0].wait_recv()
-    for half in (0, 1):
-        span = slice(4 * half, 4 * half + 4)
-        value = hubg_ref[pl.ds(c * 64 + z * 8 + 4 * half, 4)].astype(F32)
-        value = value + pairs[z, span].astype(F32)
-        for way in (0, 1):
-            hops[way, 3, half].wait_recv()
-            value = value + arrive[way, 3, half].astype(F32)
-        xsum[span] = value
-    x_stage[...] = xsum[...].astype(BF)
-    rx = [
-        go(
-            remote(
-                x_stage.at[pl.ds(lax.rem(x + o, NX) * HB, HB)],
-                x_got.at[o - 1],
-                rx_send.at[o - 1],
-                rx_recv.at[o - 1],
-                device(z, x + o, c, f),
-            )
-        )
-        for o in range(1, NX)
-    ]
+    for copy in bz:
+        copy.wait_recv()
+    value = bsum[z]
+    for o in range(1, NZ):
+        value = value + bz_got[o - 1].astype(F32)
+    sum_ref[:, FD // 2 :] = value
+    for copy in rx:
+        copy.wait_recv()
+    value = xsum[pl.ds(x * HB, HB)]
+    for o in range(1, NX):
+        value = value + x_got[o - 1].astype(F32)
+    sum_ref[:, 0 : FD // 2] = value
 
     for w in (0, 1):
         y1[w].wait_recv()
@@ -753,35 +848,21 @@
             value = value + y_last[w, half, 0:GR].astype(F32)
         logits_ref[:, cols] = value.astype(BF)
 
-    for copy in rx:
-        copy.wait_recv()
-    summed = xsum[pl.ds(x * HB, HB)]
-    for o in range(1, NX):
-        summed = summed + x_got[o - 1].astype(F32)
-    for b in range(NB):
-        cols = slice(b * BLK, (b + 1) * BLK)
-        value = out_ref[:, cols]
-        for i in range(HB):
-            value = jnp.where(hub_ref[0, i] == b, value + summed[i], value)
-        out_ref[:, cols] = value
-
     @pl.when(f != group)
     def _():
         move.wait()
 
-    turned = jnp.concatenate([g_final[...], jnp.zeros((BLK - 8, BLK), F32)], axis=0).T
-    gself_ref[...] = turned[0:GR, 0:4]
-    gneigh_ref[...] = turned[0:GR, 4:8]
+    score_ref[...] = g_final[...]
     for copy in sent:
         copy.wait_send()
 
 
-def sage(hub_blocks, tiles, hidden, rows, src_row, src_col, counts, gl, w_self, w_neigh):
+def sage(hub_blocks, tiles, hidden, rows, src, counts, gl, w_self, w_neigh):
     dma = pltpu.SemaphoreType.DMA
     outs = (
         jax.ShapeDtypeStruct((GR, ROWS_DEV), BF),
-        jax.ShapeDtypeStruct((GR, 4), F32),
-        jax.ShapeDtypeStruct((GR, 4), F32),
+        jax.ShapeDtypeStruct((8, BLK), F32),
+        jax.ShapeDtypeStruct((HB, FD, BLK), F32),
         jax.ShapeDtypeStruct((FD, ROWS_DEV), F32),
     )
 
@@ -791,7 +872,7 @@
     return pl.pallas_call(
         sage_kernel,
         out_shape=outs,
-        in_specs=[spec(pltpu.SMEM), spec(pl.ANY)] + [spec()] * 8,
+        in_specs=[spec(pltpu.SMEM), spec(pl.ANY)] + [spec()] * 7,
         out_specs=(spec(),) * 4,
         scratch_shapes=[
             VM((NB, TPB, BLK, BLK), BF),
@@ -824,11 +905,16 @@
             VM((2, GP, HALF), BF),
             VM((2, 2, GP, HALF), BF),
             VM((NZ, 8, FD, BLK), BF),
-            VM((2, 4, 2, 4, FD, BLK), BF),
-            VM((2, 4, 2, 4, FD, BLK), BF),
-            VM((8, FD, BLK), BF),
-            VM((NX - 1, HB, FD, BLK), BF),
-            VM((8, FD, BLK), F32),
+            VM((2, 4, 2, 4, FD // 2, BLK), BF),
+            VM((2, 4, 2, 4, FD // 2, BLK), BF),
+            VM((8, FD // 2, BLK), BF),
+            VM((NX - 1, HB, FD // 2, BLK), BF),
+            VM((8, FD // 2, BLK), F32),
+            VM((NX - 1, NZ, HB, FD // 2, BLK), BF),
+            VM((NX - 1, NZ, HB, FD // 2, BLK), BF),
+            VM((NZ, HB, FD // 2, BLK), F32),
+            VM((NZ, HB, FD // 2, BLK), BF),
+            VM((NZ - 1, HB, FD // 2, BLK), BF),
             VM((NX, NZ, CAP, BLK), BF),
             VM((NZ, NX, CAP, BLK), BF),
             VM((NZ, NX, CAP, BLK), BF),
@@ -856,6 +942,8 @@
         + both(3)
         + both(3)
         + both(7)
+        + both(3)
+        + both(7)
         + [dma, dma]
         + [dma, dma]
         + both(3)
@@ -864,7 +952,33 @@
         compiler_params=pltpu.CompilerParams(
             collective_id=0, has_side_effects=True, vmem_limit_bytes=60 << 20
         ),
-    )(hub_blocks, tiles, hidden, rows, src_row, src_col, counts, gl, w_self, w_neigh)
+    )(hub_blocks, tiles, hidden, rows, src, counts, gl, w_self, w_neigh)
+
+
+def finish_kernel(hub_ref, out_in, sum_in, logits_in, score_in, logits, gself, gneigh, out):
+    out[...] = out_in[...]
+    for i in range(HB):
+        start = pl.multiple_of(hub_ref[0, i] * BLK, BLK)
+        out[:, pl.ds(start, BLK)] += sum_in[i]
+    logits[...] = logits_in[...]
+    gself[...] = score_in[0:4, 0:GR]
+    gneigh[...] = score_in[4:8, 0:GR]
+
+
+def finish(hub_blocks, out, hub_sum, logits, score):
+    outs = (
+        jax.ShapeDtypeStruct((GR, ROWS_DEV), BF),
+        jax.ShapeDtypeStruct((4, GR), F32),
+        jax.ShapeDtypeStruct((4, GR), F32),
+        jax.ShapeDtypeStruct((FD, ROWS_DEV), F32),
+    )
+    return pl.pallas_call(
+        finish_kernel,
+        out_shape=outs,
+        in_specs=[spec(pltpu.SMEM)] + [spec()] * 4,
+        out_specs=(spec(),) * 4,
+        compiler_params=pltpu.CompilerParams(vmem_limit_bytes=60 << 20),
+    )(hub_blocks, out, hub_sum, logits, score)
 
 
 def local(
@@ -878,22 +992,19 @@
     weight_neigh,
     grad_logits,
 ):
-    rows = halo_rows.reshape(1, PARTS * CAP)
-    hub = tile_src - HUB0
-    moved = HUB0 + hub // 2 % 2 * 64 + hub // 16 * 8 + hub // 4 % 4 * 2 + hub % 2
-    src = jnp.where(tile_src < HUB0, tile_src, moved)
-    return sage(
+    logits, score, hub_sum, out = sage(
         hub_blocks,
         tiles,
         hidden,
-        rows,
-        src.reshape(1, TILES),
-        src.reshape(TILES, 1),
+        halo_rows[0].T,
+        tile_src.T,
         halo_counts,
         grad_logits,
         weight_self,
         weight_neigh,
     )
+    logits, gself, gneigh, out = finish(hub_blocks, out, hub_sum, logits, score)
+    return logits, gself.T, gneigh.T, out
 
 
 def solution(mesh):

time: 87.6 us -> 77 us (0.88)
  local copies, waits for them, and re-layouts: 9.82 us -> 0 us
    unnamed x3 -> x0, local copies, waits for them, and re-layouts: 4.81 us -> none
    pallas_call x2 -> x0, local copies, waits for them, and re-layouts: 2.78 us -> none  [sage(): pl.pallas_call(sage_kernel, out_shape=outs, in_specs=[spec(pltpu.SMEM), s...]
    pallas_call x0 -> x1, Pallas kernels: none -> 2.55 us  [finish(): pl.pallas_call(finish_kernel, out_shape=outs, in_specs=[spec(pltpu.SMEM)]...]
    pallas_call x1, Pallas kernels: 76 us -> 73.7 us  [sage(): pl.pallas_call(sage_kernel, out_shape=outs, in_specs=[spec(pltpu.SMEM), s...]
    reshape x3 -> x0, local copies, waits for them, and re-layouts: 2.14 us -> none  [the longest x1 0.79 us: local(): src.reshape(TILES, 1)]
where the time goes in v5:
time: 77 us; the launch traced here: 76.9 us
  Pallas kernels  76.2 us (99%)
    pallas_call x1, Pallas kernels, sage(): pl.pallas_call(sage_kernel, out_shape=outs, in_specs=[spec(pltpu.SMEM), s...  73.7 us
    pallas_call x1, Pallas kernels, finish(): pl.pallas_call(finish_kernel, out_shape=outs, in_specs=[spec(pltpu.SMEM)]...  2.55 us

profile of v5, /device:TPU:16, one launch (start us, length us, event | category | flops | bytes accessed | tf_op | source)
XLA Modules:
  0.0 76.9 jit_solution(11461554049288174699)
XLA Ops:
  0.6 73.7 %shard_map.120 = (bf16[43,4096]{1,0:T(8,128)(2,1)}, f32[8,128]{1,0:T(8,128)}, f32[2,64,128]{2,1,0:T(8,128)}, f32[64,4096]{1,0:T(8,128)}) custom-call(s32[1,2]{1,0:T(1,128)} %hub_ref.3, bf16[32,12,128,128]{3,2,1,0:T(8,128)(2,1)} %tiles_hbm.1, bf16[64,4096]{1,0:T(8,128)(2,1)} %hidden_ref.1, s32[16,64]{1,0:T(8,128)} %bitcast.6, s32[12,32]{1,0:T(8,128)} %bitcast.7, ...), custom_call_target="tpu_custom_call" | custom-call | tf_op jit(solution)/shard_map/pallas_call | solution.py:872
  74.3 2.6 %shard_map.121 = (bf16[43,4096]{1,0:T(8,128)(2,1)}, f32[4,43]{1,0:T(4,128)}, f32[4,43]{1,0:T(4,128)}, f32[64,4096]{1,0:T(8,128)}) custom-call(s32[1,2]{1,0:T(1,128)} %hub_ref.3, f32[64,4096]{1,0:T(8,128)} %get-tuple-element.12.out_in, f32[2,64,128]{2,1,0:T(8,128)} %get-tuple-element.13.sum_in, bf16[43,4096]{1,0:T(8,128)(2,1)} %get-tuple-element.14.logits_in, ...), custom_call_target="tpu_custom_call" | custom-call | tf_op jit(solution)/shard_map/pallas_call | solution.py:975

commit v6 on v5

--- a/solution.py
+++ b/solution.py
@@ -489,7 +489,7 @@
     def columns(step):
         return pl.ds(pl.multiple_of(step * WIDE, WIDE), WIDE)
 
-    @pl.loop(0, NB // 2)
+    @pl.loop(0, NB // 2, unroll=4)
     def _(step):
         gl = gl_ref[:, :, columns(step)].reshape(NF * GP, WIDE)
         both = jnp.dot(wt[...], gl, preferred_element_type=F32)
@@ -516,9 +516,13 @@
     def returned(source):
         return jnp.where(idx[4, source] == 1, runs[entry(idx, 3, source, PAIRS - 1)], 0.0)
 
-    @pl.loop(0, PARTS * HB)
-    def _(h):
-        hubg_ref[h] = returned(HUB0 + h).astype(BF)
+    def collect(core):
+        @pl.loop(0, PARTS * HB // NC, unroll=8)
+        def _(h):
+            at = core * (PARTS * HB // NC) + h
+            hubg_ref[at] = returned(HUB0 + at).astype(BF)
+
+    collect(1 - c)
 
     def hub_rows(core, plane):
         return pl.ds(core * 64 + plane * 8, 8)
@@ -536,6 +540,7 @@
                 pair,
             )
         )
+    collect(c)
     for k in range(NZ):
         block = (returned(NB + k) * live[0:1, k * BLK : (k + 1) * BLK]).astype(BF)
         zero = jnp.zeros_like(block)
@@ -605,7 +610,7 @@
     for o in range(1, NX):
         column_o = lax.rem(x + o, NX)
 
-        @pl.loop(0, NZ)
+        @pl.loop(0, NZ, unroll=NZ)
         def _(plane):
             b_stage[o - 1, plane] = hub_part(plane, column_o * HB, HB, 1).astype(BF)
 
@@ -626,7 +631,7 @@
             hc_wait(k, half)
 
     def forward(part):
-        @pl.loop(part * (NB // 8), (part + 1) * (NB // 8))
+        @pl.loop(part * (NB // 8), (part + 1) * (NB // 8), unroll=2)
         def _(step):
             gl = gl_ref[:, :, columns(step)].reshape(NF * GP, WIDE)
             means = []
@@ -697,7 +702,7 @@
     for copy in bx:
         copy.wait_recv()
 
-    @pl.loop(0, NZ)
+    @pl.loop(0, NZ, unroll=NZ)
     def _(plane):
         value = hub_part(plane, x * HB, HB, 1)
         for o in range(1, NX):

time: 77 us -> 73.9 us (0.960)
  Pallas kernels: 76.2 us -> 73.1 us
    pallas_call x1, Pallas kernels: 73.7 us -> 70.6 us  [sage(): pl.pallas_call(sage_kernel, out_shape=outs, in_specs=[spec(pltpu.SMEM), s...]
where the time goes in v6:
time: 73.9 us; the launch traced here: 73.8 us
  Pallas kernels  73.1 us (99%)
    pallas_call x1, Pallas kernels, sage(): pl.pallas_call(sage_kernel, out_shape=outs, in_specs=[spec(pltpu.SMEM), s...  70.6 us
    pallas_call x1, Pallas kernels, finish(): pl.pallas_call(finish_kernel, out_shape=outs, in_specs=[spec(pltpu.SMEM)]...  2.55 us

profile of v6, /device:TPU:16, one launch (start us, length us, event | category | flops | bytes accessed | tf_op | source)
XLA Modules:
  0.0 73.8 jit_solution(14296480881845020243)
XLA Ops:
  0.6 70.6 %shard_map.120 = (bf16[43,4096]{1,0:T(8,128)(2,1)}, f32[8,128]{1,0:T(8,128)}, f32[2,64,128]{2,1,0:T(8,128)}, f32[64,4096]{1,0:T(8,128)}) custom-call(s32[1,2]{1,0:T(1,128)} %hub_ref.3, bf16[32,12,128,128]{3,2,1,0:T(8,128)(2,1)} %tiles_hbm.1, bf16[64,4096]{1,0:T(8,128)(2,1)} %hidden_ref.1, s32[16,64]{1,0:T(8,128)} %bitcast.6, s32[12,32]{1,0:T(8,128)} %bitcast.7, ...), custom_call_target="tpu_custom_call" | custom-call | tf_op jit(solution)/shard_map/pallas_call | solution.py:877
  71.2 2.6 %shard_map.121 = (bf16[43,4096]{1,0:T(8,128)(2,1)}, f32[4,43]{1,0:T(4,128)}, f32[4,43]{1,0:T(4,128)}, f32[64,4096]{1,0:T(8,128)}) custom-call(s32[1,2]{1,0:T(1,128)} %hub_ref.3, f32[64,4096]{1,0:T(8,128)} %get-tuple-element.12.out_in, f32[2,64,128]{2,1,0:T(8,128)} %get-tuple-element.13.sum_in, bf16[43,4096]{1,0:T(8,128)(2,1)} %get-tuple-element.14.logits_in, ...), custom_call_target="tpu_custom_call" | custom-call | tf_op jit(solution)/shard_map/pallas_call | solution.py:980
